TPU v7x, 128 devices: a whole 4x4x4 slice. The times are simulated.
128 devices in a mesh: batch: 16 (over y, x), seq: 8 (over z, core).
Axes of the slice: x: 4, y: 4, z: 4, core: 2. Of those that a mesh axis runs over, the one named last changes fastest.
Arguments:
- block_input: bfloat16 [64, 1024, 768], P('batch', 'seq'), may hold values from -6 to 6
- token_ids: int32 [64, 1024], P('batch', 'seq'), may hold values from 0 to 8007, as said below
- hash_table: int32 [8008], replicated, may hold values from 0 to 15
- doc_lengths: int32 [64, 8], P('batch'), may hold values from 1 to 256, 1024 in all within a row
- turn_mask: int32 [64, 1024], P('batch', 'seq'), may hold values 0 or 1
- attn_norm_gain: float32 [768], replicated, may hold values from 0.5 to 1.5
- attn_norm_bias: float32 [768], replicated, may hold values from -3 to 3
- qkv_weight: bfloat16 [768, 2304], replicated, may hold values from -0.21875 to 0.21875
- proj_weight: bfloat16 [768, 768], replicated, may hold values from -1.75 to 1.75
- ffn_norm_gain: float32 [768], replicated, may hold values from 0.5 to 1.5
- ffn_norm_bias: float32 [768], replicated, may hold values from -3 to 3
- expert_up: bfloat16 [16, 768, 3072], P('batch'), may hold values from -0.21875 to 0.21875
- expert_down: bfloat16 [16, 3072, 768], P('batch'), may hold values from -0.109375 to 0.109375
- out_grad: bfloat16 [64, 1024, 768], P('batch', 'seq'), may hold values from -6 to 6
Outputs:
- block_output: bfloat16 [64, 1024, 768], P('batch', 'seq')
- input_grad: float32 [64, 1024, 768], P('batch', 'seq')
- attn_gain_grad: float32 [768], replicated
- attn_bias_grad: float32 [768], replicated
- qkv_grad: float32 [768, 2304], replicated
- proj_grad: float32 [768, 768], replicated
- ffn_gain_grad: float32 [768], replicated
- ffn_bias_grad: float32 [768], replicated
- up_grad: float32 [16, 768, 3072], P('batch', None, 'seq')
- down_grad: float32 [16, 3072, 768], P('batch', 'seq')
- expert_counts: int32 [16], replicated
- received_counts: int32 [16, 8, 16], P('batch', 'seq')
Inputs may be any that keep to these rules, and one draw needn't show every extreme that they name: `token_ids`: among the 512 tokens of one device (4 rows by 128 positions), at most 64 have an expert (by hash_table) equal to any one expert; in every draw one expert gets exactly 64 from every device. `doc_lengths`: the 8 lengths of a row sum to 1024; the longest of each row is exactly 256.
All inputs are finite; a program needn't handle non-finite values. No bound on the sum of `turn_mask` on one device may be relied on, other than what follows from the above.
Results may differ from a plain program's by a relative error of at most 0.0098.
Values may be sent and summed in bfloat16 or wider, within the bound.
No kernel may reach another device: no remote copies, remote signals or barrier semaphores. Data moves between devices by JAX's collectives and lax.ppermute only.
A program may use at most 192 MiB of HBM per device.

v0:
```python
import jax
import jax.numpy as jnp
from jax import lax
from jax.experimental import pallas as pl
from jax.experimental.pallas import tpu as pltpu
from jax.sharding import PartitionSpec as P

BF = jnp.bfloat16
F32 = jnp.float32
I32 = jnp.int32
EPS = 1e-05
MASKED = -1e30
HEADS = 12
HEAD_SIZE = 64
PAIRS = 6
CAP = 64
SWAP = [(i, i ^ 1) for i in range(8)]
UP_ONE = [(i, i + 1) for i in range(0, 8, 2)]
DOWN_ONE = [(i + 1, i) for i in range(0, 8, 2)]
AHEAD_TWO = [(i, i + 2) for i in range(6)]
BACK_TWO = [(i + 2, i) for i in range(6)]
HALF_ROWS = 5120
VMEM_BYTES = 63 * 1024 * 1024
GEMM_ROWS = 4608
VM = pl.BlockSpec(memory_space=pltpu.VMEM)
HB = pl.BlockSpec(memory_space=pl.ANY)
SM = pl.BlockSpec(memory_space=pltpu.SMEM)


def shape(dims, kind=BF):
    return jax.ShapeDtypeStruct(dims, kind)


def kernel_call(body, outs, args, name, flops, grid=None, in_specs=None, out_specs=None, scratch=(), aliases=None):
    moved = sum(a.size * a.dtype.itemsize for a in args) + sum(
        o.size * o.dtype.itemsize for o in outs
    )
    extra = {} if grid is None else {"grid": grid}
    return pl.pallas_call(
        body,
        out_shape=outs,
        in_specs=in_specs or [VM] * len(args),
        out_specs=out_specs or [VM] * len(outs),
        scratch_shapes=list(scratch),
        compiler_params=pltpu.CompilerParams(vmem_limit_bytes=VMEM_BYTES),
        cost_estimate=pl.CostEstimate(flops=flops, bytes_accessed=moved, transcendentals=0),
        name=name,
        input_output_aliases=aliases or {},
        **extra,
    )(*args)


def nn(a, b):
    return jnp.dot(a, b, preferred_element_type=F32)


def nt(a, b):
    return lax.dot_general(a, b, (((1,), (1,)), ((), ())), preferred_element_type=F32)


def tn(a, b):
    return lax.dot_general(a, b, (((0,), (0,)), ((), ())), preferred_element_type=F32)


def iota(dims, axis):
    return lax.broadcasted_iota(I32, dims, axis)


def row(ref):
    return ref[...].reshape(1, 768)


def column(line):
    return jnp.broadcast_to(line, (128, line.shape[1])).T[:, 0:1]


def flat_line(ref):
    return jnp.concatenate([ref[i : i + 1, :] for i in range(4)], axis=1).astype(F32)


def norm_parts(values):
    centred = values - jnp.mean(values, axis=-1, keepdims=True)
    inverse = lax.rsqrt(jnp.mean(centred * centred, axis=-1, keepdims=True) + EPS)
    return centred * inverse, inverse


def norm_back(grad, gain, unit, inverse):
    t = grad * gain
    return inverse * (
        t - jnp.mean(t, axis=-1, keepdims=True) - unit * jnp.mean(t * unit, axis=-1, keepdims=True)
    )


def route_kernel(place, tok, table, turn, grad, target_out, tally, sent):
    ids = jnp.concatenate([tok[i : i + 1, :] for i in range(4)], axis=1)
    live = flat_line(turn)
    high, low = ids >> 7, ids & 127
    picked = tn(table[...].astype(F32).astype(BF), (iota((64, 512), 0) == high).astype(F32).astype(BF))
    chosen = jnp.sum(jnp.where(iota((128, 512), 0) == low, picked, 0.0), axis=0, keepdims=True)
    member = (iota((16, 512), 0) == chosen.astype(I32)).astype(F32)
    earlier = (iota((512, 512), 0) < iota((512, 512), 1)).astype(F32).astype(BF)
    before = nn(member.astype(BF), earlier)
    slot = jnp.sum(before * member, axis=0, keepdims=True)
    target = (chosen * CAP + slot).astype(I32)
    target_out[...] = jnp.broadcast_to(target, (8, 512))
    counts = jnp.sum(member, axis=1, keepdims=True)
    tally[...] = jnp.where(iota((16, 128), 1) == place[0] * 16 + place[1], counts, 0.0)
    for i in range(4):
        placing = jnp.where(iota((256, 512), 0) + 256 * i == target, live, 0.0).astype(BF)
        sent[256 * i : 256 * (i + 1), :] = nn(placing, grad[...]).astype(BF)


def own_kernel(x, gain, bias, weight, unit_out, query, keyval):
    unit, _ = norm_parts(x[...].astype(F32))
    unit_out[...] = unit.astype(BF)
    rows = (unit * row(gain) + row(bias)).astype(BF)
    query[...] = nn(rows, weight[:, :768]).astype(BF)
    keyval[...] = nn(rows, weight[:, 768:]).astype(BF)


def head_masks(scale):
    lane = iota((1, 128), 1)
    first = jnp.where(lane < 64, scale, 0.0).astype(BF)
    second = jnp.where(lane >= 64, scale, 0.0).astype(BF)
    return first, second


def stack_heads(pair, masks):
    return jnp.concatenate([pair * masks[0], pair * masks[1]], axis=0)


def window_bias(place, lengths, r):
    lane = iota((1, 128), 1) + place[0] * 128
    end, start = jnp.int32(0), jnp.zeros((1, 128), I32)
    for j in range(8):
        end = end + lengths[r, j]
        start = jnp.where(end <= lane, end, start)
    start = start - (place[0] - 2) * 128
    key = iota((384, 128), 0)
    allowed = (key >= start) & (key <= iota((384, 128), 1) + 256)
    half = jnp.where(allowed, 0.0, MASKED)
    return jnp.concatenate([half, half], axis=1)


def join_heads(both):
    one = jnp.where(iota((128, 128), 0) < 64, both[:, :128], both[:, 128:])
    return one.T


def copies(sources, targets, sems):
    out = [
        pltpu.make_async_copy(a, b, sems.at[i]) for i, (a, b) in enumerate(zip(sources, targets))
    ]
    for copy in out:
        copy.start()
    return out


def lanes_of(p, offset=0):
    return slice(offset + 128 * p, offset + 128 * (p + 1))


def forward_kernel(
    place, lengths, gain, bias, gain_two, bias_two, target,
    behind_two, early, late, weight, keyval, query, x, proj,
    unit_halo, context_out, attended, log_out, after_out, sent,
    b2, e1, l1, w, q, xv, wp, units, rows_in, context, att, aft, snd, in_sems, out_sems,
):
    loads = copies(
        [behind_two, early, late, weight, keyval, query, x, proj],
        [b2, e1, l1, w, context.at[:, 256:384, :], q, xv, wp],
        in_sems,
    )
    scales = head_masks(HEAD_SIZE ** (-0.5))
    for copy in loads[:3]:
        copy.wait()

    def norm_row(r, carry):
        halo = jnp.concatenate([b2[r], e1[r] + l1[r]], axis=0).astype(F32)
        unit, _ = norm_parts(halo)
        units[r] = unit.astype(BF)
        rows_in[r] = (unit * row(gain) + row(bias)).astype(BF)
        return carry

    lax.fori_loop(0, 4, norm_row, 0)
    unit_copy = pltpu.make_async_copy(units, unit_halo, out_sems.at[0])
    unit_copy.start()
    loads[3].wait()
    for j in range(3):
        cols = slice(512 * j, 512 * (j + 1))
        fresh = nn(rows_in[...].reshape(1024, 768), w[:, 768 + 512 * j : 768 + 512 * (j + 1)])
        context[:, 0:256, cols] = fresh.astype(BF).reshape(4, 256, 512)
    for copy in loads[4:6]:
        copy.wait()
    context_copy = pltpu.make_async_copy(context, context_out, out_sems.at[1])
    context_copy.start()

    def one_row(r, carry):
        mask = window_bias(place, lengths, r)
        pairs = range(PAIRS)
        stacked = [stack_heads(q[r, :, lanes_of(p)], scales) for p in pairs]
        scores = [nt(context[r, :, lanes_of(p)], stacked[p]) + mask for p in pairs]
        tops = [jnp.max(a, axis=0, keepdims=True) for a in scores]
        weights = [jnp.exp(a - t) for a, t in zip(scores, tops)]
        totals = [jnp.sum(a, axis=0, keepdims=True) for a in weights]
        shares = [(a * (1.0 / t)).astype(BF) for a, t in zip(weights, totals)]
        mixed = [tn(context[r, :, lanes_of(p, 768)], shares[p]) for p in pairs]
        for p in pairs:
            log_out[r, p : p + 1, :] = tops[p] + jnp.log(totals[p])
            att[r, :, lanes_of(p)] = join_heads(mixed[p]).astype(BF)
        return carry

    lax.fori_loop(0, 4, one_row, 0)
    att_copy = pltpu.make_async_copy(att, attended, out_sems.at[2])
    att_copy.start()
    loads[6].wait()
    loads[7].wait()
    after = xv[...].reshape(512, 768).astype(F32) + nn(att[...].reshape(512, 768), wp[...])
    aft[...] = after
    after_copy = pltpu.make_async_copy(aft, after_out, out_sems.at[3])
    after_copy.start()
    unit, _ = norm_parts(after)
    rows = (unit * row(gain_two) + row(bias_two)).astype(BF)
    sends = []
    for i in range(2):
        part = slice(512 * i, 512 * (i + 1))
        placing = (iota((512, 512), 0) + 512 * i == target[0:1, :]).astype(F32).astype(BF)
        snd[part, :] = nn(placing, rows).astype(BF)
        sends.append(pltpu.make_async_copy(snd.at[part], sent.at[part], out_sems.at[4 + i]))
        sends[-1].start()
    for copy in [unit_copy, context_copy, att_copy, after_copy] + sends:
        copy.wait()


def active_grad_kernel(grad, down, out):
    out[0] = nt(grad[...], down[...]).astype(BF)


def gelu_both(v):
    c = 0.7978845608028654
    square = v * v
    p = c + (c * 0.044715) * square
    gate = 0.5 + 0.5 * jnp.tanh(v * p)
    value = v * gate
    return value, gate + value * (1.0 - gate) * (6.0 * p - 4.0 * c)


def expert_kernel(x, up, raw, active, hidden_grad, back, total):
    step = pl.program_id(0)

    @pl.when(step == 0)
    def _():
        total[...] = jnp.zeros_like(total)

    parts = [slice(256 * r, 256 * (r + 1)) for r in range(4)]
    hidden = [nn(x[rows, :], up[...]) for rows in parts]
    lows = []
    for rows, v in zip(parts, hidden):
        value, slope = gelu_both(v)
        active[0, rows, :] = value.astype(BF)
        low = (raw[0, rows, :].astype(F32) * slope).astype(BF)
        hidden_grad[0, rows, :] = low
        lows.append(low)
    for rows, low in zip(parts, lows):
        total[rows, :] += nt(low, up[...])

    @pl.when(step == pl.num_programs(0) - 1)
    def _():
        back[...] = total[...].astype(BF)


def turn_kernel(unit, unit_halo, out):
    out[0:768, 0:512] = unit[...].T
    out[0:768, 512:1536] = unit_halo[...].T
    out[768:784, :] = jnp.ones((16, 1536), BF)


def weight_kernel(x, grad, active, hidden_grad, down, out, parts, x_t, grad_t, total):
    step = pl.program_id(0)

    @pl.when(step == 0)
    def _():
        total[...] = jnp.zeros_like(total)
        x_t[...] = x[...].T
        grad_t[...] = grad[...].T

    total[...] += nn(active[0], down[...])
    one = nn(x_t[...], hidden_grad[0]).astype(BF)
    two = nn(grad_t[...], active[0]).astype(BF)
    for j in range(2):
        parts[j, :768, :] = one[:, 384 * j : 384 * (j + 1)]
        parts[j, 768:, :] = two[:, 384 * j : 384 * (j + 1)]

    @pl.when(step == pl.num_programs(0) - 1)
    def _():
        out[...] = total[...].astype(BF)


def output_kernel(after, target, returned, out):
    placing = (iota((512, 1024), 1).astype(F32) == column(target[0:1, :].astype(F32))).astype(F32).astype(BF)
    out[...] = (after[...] + nn(placing, returned[...])).astype(BF)


def fill_halves(
    turned, query_grad, context_grad, weight, gain, bias, proj_part, terms_two, tally,
    out, gain_wide, bias_wide, gain_sum, bias_sum,
):
    gain_wide[...] = jnp.broadcast_to(row(gain), (256, 768)).T
    bias_wide[...] = jnp.broadcast_to(row(bias), (256, 768)).T

    def finish(block, both):
        body, sums = both[0:768], both[768:769]
        half, step = block // 6, block % 6
        out[half, 768 * step : 768 * (step + 1), :] = (
            gain_wide[...] * body + bias_wide[...] * sums
        ).astype(BF)
        wide = weight[:, 256 * block : 256 * (block + 1)].astype(F32)
        if block == 0:
            gain_sum[...] = wide * body
            bias_sum[...] = wide * sums
        else:
            gain_sum[...] += wide * body
            bias_sum[...] += wide * sums

    for j in range(3):
        finish(j, nn(turned[:, 0:512], query_grad[:, 256 * j : 256 * (j + 1)]))
        out[1, 768 * (3 + j) : 768 * (4 + j), :] = proj_part[j]
    for j in range(6):
        finish(3 + j, nn(turned[...], context_grad[:, 256 * j : 256 * (j + 1)]))

    columns = jnp.concatenate(
        [
            jnp.broadcast_to(jnp.sum(gain_sum[...], axis=1, keepdims=True), (768, 128)),
            jnp.broadcast_to(jnp.sum(bias_sum[...], axis=1, keepdims=True), (768, 128)),
        ],
        axis=1,
    ).T
    out[:, GEMM_ROWS:, :] = jnp.zeros((2, HALF_ROWS - GEMM_ROWS, 256), BF)
    for t in range(3):
        lanes = slice(256 * t, 256 * (t + 1))
        block = jnp.concatenate(
            [columns[0:1, lanes], columns[128:129, lanes], terms_two[:, lanes], jnp.zeros((12, 256), F32)],
            axis=0,
        )
        out[0, GEMM_ROWS + 16 * t : GEMM_ROWS + 16 * t + 16, :] = block.astype(BF)
    out[0, GEMM_ROWS + 48 : GEMM_ROWS + 64, 0:128] = tally[...].astype(BF)


def backward_kernel(
    place, lengths, gain_two, gain, bias, target, turn, log_total, tally,
    back, after, grad, proj, attended, query, context, turned, weight,
    after_grad, query_grad, own_grad, input_two, input_one, keep, away,
    bk, af, gr, wp, att, q, ctx, tu, w, ag, do, dq, cg, pp, ip, out,
    gain_wide, bias_wide, gain_sum, bias_sum, terms, in_sems, out_sems,
):
    loads = copies(
        [back, after, grad, proj, attended, query, context, turned, weight],
        [bk, af, gr, wp, att, q, ctx, tu, w],
        in_sems,
    )
    scales = head_masks(HEAD_SIZE ** (-0.5))
    ones = head_masks(1.0)
    placing = (iota((512, 1024), 1).astype(F32) == column(target[0:1, :].astype(F32))).astype(F32).astype(BF)
    live = column(flat_line(turn))
    loads[0].wait()
    normed_grad = nn(placing, bk[...])
    loads[1].wait()
    unit, inverse = norm_parts(af[...])
    terms[0:1, :] = jnp.sum(normed_grad * unit, axis=0, keepdims=True)
    terms[1:2, :] = jnp.sum(normed_grad, axis=0, keepdims=True)
    loads[2].wait()
    total = gr[...].astype(F32) * live + norm_back(normed_grad, row(gain_two), unit, inverse)
    ag[...] = total
    stores = [pltpu.make_async_copy(ag, after_grad, out_sems.at[0])]
    stores[0].start()
    low = total.astype(BF)
    loads[3].wait()
    do[...] = nt(low, wp[...]).astype(BF).reshape(4, 128, 768)
    loads[4].wait()
    mixed = nn(att[...].T, low).astype(BF)
    for j in range(3):
        pp[j] = mixed[:, 256 * j : 256 * (j + 1)]
    loads[5].wait()
    loads[6].wait()

    def one_row(r, carry):
        mask = window_bias(place, lengths, r)
        pairs = range(PAIRS)
        stacked = [stack_heads(q[r, :, lanes_of(p)], scales) for p in pairs]
        grads = [stack_heads(do[r, :, lanes_of(p)], ones) for p in pairs]
        scores = [nt(ctx[r, :, lanes_of(p)], stacked[p]) for p in pairs]
        share_grads = [nt(ctx[r, :, lanes_of(p, 768)], grads[p]) for p in pairs]
        shares = [jnp.exp(scores[p] + mask - log_total[r, p : p + 1, :]) for p in pairs]
        sums = [jnp.sum(a * b, axis=0, keepdims=True) for a, b in zip(shares, share_grads)]
        score_grads = [(a * (b - c)).astype(BF) for a, b, c in zip(shares, share_grads, sums)]
        key_grads = [nn(score_grads[p], stacked[p]).astype(BF) for p in pairs]
        value_grads = [nn(shares[p].astype(BF), grads[p]).astype(BF) for p in pairs]
        turned_grads = [tn(ctx[r, :, lanes_of(p)], score_grads[p]) for p in pairs]
        halo = pl.ds(pl.multiple_of(512 + r * 256, 256), 256)
        own = pl.ds(pl.multiple_of(r * 128, 128), 128)
        for p in pairs:
            cg[halo, lanes_of(p)] = key_grads[p][:256]
            cg[own, lanes_of(p)] = key_grads[p][256:]
            cg[halo, lanes_of(p, 768)] = value_grads[p][:256]
            cg[own, lanes_of(p, 768)] = value_grads[p][256:]
            dq[own, lanes_of(p)] = (join_heads(turned_grads[p]) * HEAD_SIZE ** (-0.5)).astype(BF)
        return carry

    lax.fori_loop(0, 4, one_row, 0)
    loads[7].wait()
    loads[8].wait()

    def store(source, target):
        stores.append(pltpu.make_async_copy(source, target, out_sems.at[len(stores)]))
        stores[-1].start()

    store(dq, query_grad)
    store(cg.at[0:512], own_grad)
    ip[...] = nt(cg[512:1536, :], w[:, 768:]).astype(BF).reshape(4, 256, 768)
    store(ip.at[:, 0:128], input_two)
    store(ip.at[:, 128:256], input_one)
    fill_halves(
        tu, dq, cg, w, gain, bias, pp, terms, tally, out, gain_wide, bias_wide, gain_sum, bias_sum
    )
    core = place[0] % 2

    @pl.when(core == 0)
    def _():
        pltpu.make_async_copy(out.at[0], keep, out_sems.at[5]).start()
        pltpu.make_async_copy(out.at[1], away, out_sems.at[6]).start()

    @pl.when(core == 1)
    def _():
        pltpu.make_async_copy(out.at[1], keep, out_sems.at[5]).start()
        pltpu.make_async_copy(out.at[0], away, out_sems.at[6]).start()

    for copy in stores:
        copy.wait()
    pltpu.make_async_copy(out.at[0], keep, out_sems.at[5]).wait()
    pltpu.make_async_copy(out.at[1], away, out_sems.at[6]).wait()


def place_half(half, data, qkv, proj, stage, sems):
    for j in range(6):
        lanes = slice(256 * (j % 3), 256 * (j % 3 + 1))
        stage[j // 3, :, lanes] = data[768 * j : 768 * (j + 1), :].astype(F32)

    @pl.when(half == 0)
    def _():
        one = pltpu.make_async_copy(stage.at[0], qkv.at[:, 0:768], sems.at[0])
        two = pltpu.make_async_copy(stage.at[1], qkv.at[:, 768:1536], sems.at[1])
        one.start()
        two.start()
        one.wait()
        two.wait()

    @pl.when(half == 1)
    def _():
        one = pltpu.make_async_copy(stage.at[0], qkv.at[:, 1536:2304], sems.at[0])
        two = pltpu.make_async_copy(stage.at[1], proj, sems.at[1])
        one.start()
        two.start()
        one.wait()
        two.wait()


def finish_mine_kernel(place, mine, qkv, proj, stage, sems):
    place_half(place[0] % 2, mine, qkv, proj, stage, sems)


def finish_other_kernel(
    place, other, tail, qkv_in, proj_in, qkv, proj, gain_one, bias_one, gain_two, bias_two, counts, received, stage, sems
):
    both = tail[...].astype(F32) + other[GEMM_ROWS:, :].astype(F32)
    for i, out in enumerate([gain_one, bias_one, gain_two, bias_two]):
        line = jnp.concatenate([both[16 * t + i : 16 * t + i + 1, :] for t in range(3)], axis=1)
        out[...] = line.reshape(768)
    every = both[48:64, 0:128]
    counts[...] = nt(jnp.ones((8, 128), BF), every.astype(BF))[0:1, :].astype(I32).reshape(16)
    chosen = (iota((16, 128), 0) == place[1]) & ((iota((16, 128), 1) >> 4) == place[0])
    mine = jnp.where(chosen, every, 0.0).astype(BF)
    fold = ((iota((128, 16), 0) & 15) == iota((128, 16), 1)).astype(F32).astype(BF)
    received[0] = jnp.sum(nn(mine, fold), axis=0, keepdims=True).astype(I32)
    place_half(1 - place[0] % 2, other, qkv, proj, stage, sems)


def expert_sum_kernel(parts, up, down):
    up[0] = parts[0, :768, :].astype(F32)
    down[0] = parts[0, 768:, :].astype(F32).T


def input_grad_kernel(
    even, gain, query_grad, own_grad, weight, x, from_one, from_two, after_grad, out,
    dq, og, w, xv, one, two, ag, in_sems,
):
    loads = copies(
        [weight, query_grad, own_grad, x, from_one, from_two, after_grad], [w, dq, og, xv, one, two, ag], in_sems
    )
    for copy in loads[:3]:
        copy.wait()
    total = nt(dq[...], w[:, :768]) + nt(og[...], w[:, 768:])
    for copy in loads[3:]:
        copy.wait()
    unit, inverse = norm_parts(xv[...].astype(F32))
    total = total + two[...].astype(F32) + even[0] * one[...].astype(F32)
    out[...] = ag[...] + norm_back(total, row(gain), unit, inverse)


PAIR_ONE = [b ^ 1 for b in range(4)]
PAIR_TWO = [b ^ 3 for b in range(4)]
PAIRS_OF = [PAIR_ONE, PAIR_TWO]
BOTH = ("batch", "seq")


def by_core(even_move, odd_move):
    pairs = []
    for b in range(16):
        for s in range(8):
            x, y = (even_move, odd_move)[s % 2](b & 3, b >> 2)
            pairs.append((b * 8 + s, (y * 4 + x) * 8 + s))
    return pairs


def first_pairs(pair):
    return by_core(lambda x, y: (pair[x], y), lambda x, y: (x, pair[y]))


def second_step(d):
    return by_core(lambda x, y: (x, (y + d) & 3), lambda x, y: ((x + d) & 3, y))


def along_z(d):
    return [(s, (s + 2 * d) & 7) for s in range(8)]


def pick(array, index):
    return lax.dynamic_index_in_dim(array, index, 0, keepdims=False)


def part_of(array, index):
    return lax.dynamic_index_in_dim(array, index % 4, 1, keepdims=False)


def sum_start(keep, got):
    seq, place = lax.axis_index("seq"), lax.axis_index("batch")
    core, x, y = seq % 2, place % 4, place // 4
    one, two = jnp.where(core == 0, x, y), jnp.where(core == 0, y, x)
    bits = [(one & 1) ^ (one >> 1), one >> 1]
    size = HALF_ROWS // 4

    def part(stream, bit):
        at = (stream * 2 + bit) * size
        return rows_at(keep, at, size).astype(F32) + rows_at(got, at, size).astype(F32)

    moved = [
        lax.ppermute(part(i, 1 - bits[i]).astype(BF), BOTH, first_pairs(PAIRS_OF[i])) for i in range(2)
    ]
    return bits, two, part, moved


def rows_at(array, at, size):
    return lax.dynamic_slice(array, (at, 0), (size, array.shape[1]))


def pair_gather(chunks, bits, pairs):
    moved = [lax.ppermute(data, BOTH, first_pairs(pair)) for pair, data in zip(pairs, chunks)]
    return [
        jnp.where(bit == 0, jnp.stack([a, b]), jnp.stack([b, a])).reshape(-1, a.shape[1])
        for bit, a, b in zip(bits, chunks, moved)
    ]


def sum_finish(bits, place, part, moved, beside):
    size = HALF_ROWS // 8
    sums = [part(i, bits[i]) + moved[i].astype(F32) for i in range(2)]
    sent = [rows_at(sums[i], (1 - bits[1 - i]) * size, size).astype(BF) for i in range(2)]
    stay = [rows_at(sums[i], bits[1 - i] * size, size) for i in range(2)]
    moved = [lax.ppermute(sent[i], BOTH, first_pairs(PAIRS_OF[1 - i])) for i in range(2)]
    chunks = [(a + b.astype(F32)).astype(BF) for a, b in zip(stay, moved)]
    size, lanes = chunks[0].shape
    grouped = jnp.stack(chunks).reshape(2, 4, size // 4, lanes)
    total = part_of(grouped, place).astype(F32)
    for d in (2, 1, 3):
        total = total + lax.ppermute(part_of(grouped, place + d), BOTH, second_step(d)).astype(F32)
    whole = after_all(total.astype(BF), *beside[0])
    total = whole.astype(F32)
    for d in (2, 1, 3):
        total = total + lax.ppermute(whole, "seq", along_z(d)).astype(F32)
    piece = after_all(total.astype(BF), *beside[1])
    parts = [piece] + [lax.ppermute(piece, BOTH, second_step(d)) for d in (1, 2, 3)]
    stack = jnp.stack(parts, axis=1)
    ordered = jnp.stack([part_of(stack, place - p + 4) for p in range(4)], axis=1).reshape(2, size, lanes)
    chunks = pair_gather([ordered[0], ordered[1]], bits[::-1], PAIRS_OF[::-1])
    chunks[0] = after_all(chunks[0], *beside[2])
    chunks = pair_gather(chunks, bits, PAIRS_OF)
    return jnp.concatenate(chunks, axis=0)


def after_all(value, *others):
    return lax.optimization_barrier((value, *others))[0]


def exchange(array):
    return lax.all_to_all(
        array.reshape(16, CAP, 768), "batch", split_axis=0, concat_axis=0, tiled=True
    ).reshape(1024, 768)


def local(
    block_input, token_ids, hash_table, doc_lengths, turn_mask, attn_norm_gain, attn_norm_bias,
    qkv_weight, proj_weight, ffn_norm_gain, ffn_norm_bias, expert_up, expert_down, out_grad,
):
    seq = lax.axis_index("seq")
    owner = lax.axis_index("batch")
    odd = seq % 2
    flat = (512, 768)
    rows3 = (4, 128, 768)
    place = jnp.stack([seq, owner]).astype(I32)
    up, down = expert_up[0], expert_down[0]

    behind_two = lax.ppermute(block_input, "seq", AHEAD_TWO)
    early = lax.ppermute(block_input, "seq", UP_ONE)

    table = jnp.pad(hash_table, (0, 8192 - 8008)).reshape(64, 128)
    target, tally, grad_sent = kernel_call(
        route_kernel,
        [shape((8, 512), I32), shape((16, 128), F32), shape((1024, 768))],
        [place, token_ids, table, turn_mask, out_grad.reshape(flat)],
        "route", 10**9,
        in_specs=[SM] + [VM] * 4,
    )
    grad_rows = exchange(grad_sent)

    unit, query, keyval = kernel_call(
        own_kernel,
        [shape(flat), shape(flat), shape((512, 1536))],
        [block_input.reshape(flat), attn_norm_gain, attn_norm_bias, qkv_weight],
        "own", 18 * 10**8,
    )
    late = lax.ppermute(after_all(behind_two, query, grad_sent), "seq", DOWN_ONE)
    query, keyval = query.reshape(rows3), keyval.reshape(4, 128, 1536)

    unit_halo, context, attended, log_total, after, rows_sent = kernel_call(
        forward_kernel,
        [
            shape((4, 256, 768)), shape((4, 384, 1536)), shape(rows3), shape((4, 8, 256), F32),
            shape(flat, F32), shape((1024, 768)),
        ],
        [
            place, doc_lengths, attn_norm_gain, attn_norm_bias, ffn_norm_gain, ffn_norm_bias, target,
            behind_two, early, late, qkv_weight, keyval, query, block_input, proj_weight,
        ],
        "forward", 10**9,
        in_specs=[SM] * 2 + [VM] * 5 + [HB] * 8,
        out_specs=[HB] * 3 + [VM] + [HB] * 2,
        scratch=[
            pltpu.VMEM(rows3, BF), pltpu.VMEM(rows3, BF), pltpu.VMEM(rows3, BF), pltpu.VMEM((768, 2304), BF),
            pltpu.VMEM(rows3, BF), pltpu.VMEM(rows3, BF), pltpu.VMEM((768, 768), BF),
            pltpu.VMEM((4, 256, 768), BF), pltpu.VMEM((4, 256, 768), BF), pltpu.VMEM((4, 384, 1536), BF),
            pltpu.VMEM(rows3, BF), pltpu.VMEM(flat, F32), pltpu.VMEM((1024, 768), BF),
            pltpu.SemaphoreType.DMA((8,)), pltpu.SemaphoreType.DMA((6,)),
        ],
    )
    rows = exchange(rows_sent)

    turned = kernel_call(
        turn_kernel, [shape((784, 1536))], [unit, unit_halo.reshape(1024, 768)], "turn", 10**6
    )[0]
    tile = pl.BlockSpec((1, 1024, 768), lambda i: (i, 0, 0))
    tiled = shape((4, 1024, 768))
    whole = pl.BlockSpec((1024, 768), lambda i: (0, 0))
    raw = kernel_call(
        active_grad_kernel,
        [tiled],
        [after_all(grad_rows, turned), down],
        "active_grad", 48 * 10**8,
        grid=(4,),
        in_specs=[whole, pl.BlockSpec((768, 768), lambda i: (i, 0))],
        out_specs=[tile],
    )[0]

    active, hidden_grad, back_sent = kernel_call(
        expert_kernel,
        [tiled, tiled, shape((1024, 768))],
        [rows, up, raw],
        "expert", 97 * 10**8,
        grid=(4,),
        in_specs=[whole, pl.BlockSpec((768, 768), lambda i: (0, i)), tile],
        out_specs=[tile, tile, whole],
        scratch=[pltpu.VMEM((1024, 768), F32)],
    )
    back = exchange(back_sent)

    result, parts = kernel_call(
        weight_kernel,
        [shape((1024, 768)), shape((8, 1536, 384))],
        [rows, grad_rows, active, hidden_grad, down],
        "weights", 145 * 10**8,
        grid=(4,),
        in_specs=[
            whole,
            whole,
            tile,
            tile,
            pl.BlockSpec((768, 768), lambda i: (i, 0)),
        ],
        out_specs=[
            pl.BlockSpec((1024, 768), lambda i: (0, 0)),
            pl.BlockSpec((2, 1536, 384), lambda i: (i, 0, 0)),
        ],
        scratch=[pltpu.VMEM((768, 1024), BF), pltpu.VMEM((768, 1024), BF), pltpu.VMEM((1024, 768), F32)],
    )
    returned = exchange(result)
    parts_sum = lax.psum_scatter(after_all(parts, back), "seq", scatter_dimension=0, tiled=True)

    after_grad, query_grad, own_grad, input_two, input_one, keep, away = kernel_call(
        backward_kernel,
        [
            shape(flat, F32), shape(flat), shape((512, 1536)), shape(rows3), shape(rows3),
            shape((HALF_ROWS, 256)), shape((HALF_ROWS, 256)),
        ],
        [
            place, doc_lengths, ffn_norm_gain, attn_norm_gain, attn_norm_bias, target, turn_mask, log_total, tally,
            back, after, out_grad.reshape(flat), proj_weight, attended.reshape(flat), query, context, turned,
            qkv_weight,
        ],
        "backward", 16 * 10**9,
        in_specs=[SM] * 2 + [VM] * 7 + [HB] * 9,
        out_specs=[HB] * 7,
        scratch=[
            pltpu.VMEM((1024, 768), BF), pltpu.VMEM(flat, F32), pltpu.VMEM(flat, BF), pltpu.VMEM((768, 768), BF),
            pltpu.VMEM(flat, BF), pltpu.VMEM(rows3, BF), pltpu.VMEM((4, 384, 1536), BF),
            pltpu.VMEM((784, 1536), BF), pltpu.VMEM((768, 2304), BF), pltpu.VMEM(flat, F32), pltpu.VMEM(rows3, BF),
            pltpu.VMEM(flat, BF), pltpu.VMEM((1536, 1536), BF), pltpu.VMEM((3, 768, 256), BF),
            pltpu.VMEM((4, 256, 768), BF), pltpu.VMEM((2, HALF_ROWS, 256), BF),
            pltpu.VMEM((768, 256), F32), pltpu.VMEM((768, 256), F32), pltpu.VMEM((768, 256), F32),
            pltpu.VMEM((768, 256), F32), pltpu.VMEM((2, 768), F32),
            pltpu.SemaphoreType.DMA((9,)), pltpu.SemaphoreType.DMA((7,)),
        ],
    )
    got = lax.ppermute(after_all(away, returned), "seq", SWAP)
    bits, turn, part, streams = sum_start(keep, got)

    from_one = lax.ppermute(input_one, "seq", SWAP)
    passed = jnp.where(odd == 1, input_two + from_one, input_two)
    from_two = lax.ppermute(passed, "seq", BACK_TWO)
    even = (1 - odd).astype(F32).reshape(1)
    input_grad = kernel_call(
        input_grad_kernel,
        [shape(flat, F32)],
        [
            even, attn_norm_gain, query_grad, own_grad, qkv_weight, block_input.reshape(flat),
            from_one.reshape(flat), from_two.reshape(flat), after_grad,
        ],
        "input_grad", 3 * 10**9,
        in_specs=[SM, VM] + [HB] * 7,
        scratch=[
            pltpu.VMEM(flat, BF), pltpu.VMEM((512, 1536), BF), pltpu.VMEM((768, 2304), BF), pltpu.VMEM(flat, BF),
            pltpu.VMEM(flat, BF), pltpu.VMEM(flat, BF), pltpu.VMEM(flat, F32), pltpu.SemaphoreType.DMA((7,)),
        ],
    )[0]
    block_output = kernel_call(
        output_kernel, [shape(flat)], [after, target, returned], "output", 8 * 10**8
    )[0]
    up_sum, down_sum = kernel_call(
        expert_sum_kernel,
        [shape((1, 768, 384), F32), shape((1, 384, 768), F32)],
        [parts_sum], "expert_sum", 10**6,
    )
    mine = sum_finish(bits, turn, part, streams, ([from_two], [block_output, up_sum], [input_grad]))
    other = lax.ppermute(mine, "seq", SWAP)
    sums = [shape((768, 2304), F32), shape((768, 768), F32)]
    away_spec = [pl.BlockSpec(memory_space=pl.ANY)] * 2
    landing = [pltpu.VMEM((2, 768, 768), F32), pltpu.SemaphoreType.DMA((2,))]
    qkv_half, proj_half = kernel_call(
        finish_mine_kernel, sums, [place, mine], "finish_mine", 10**6,
        in_specs=[SM, VM], out_specs=away_spec, scratch=landing,
    )
    line = shape((768,), F32)
    qkv_sum, proj_sum, *rest = kernel_call(
        finish_other_kernel,
        sums + [line] * 4 + [shape((16,), I32), shape((1, 1, 16), I32)],
        [place, other, mine[GEMM_ROWS:], qkv_half, proj_half],
        "finish_other", 10**6,
        in_specs=[SM, VM, VM] + away_spec, out_specs=away_spec + [VM] * 6, scratch=landing,
        aliases={3: 0, 4: 1},
    )
    return (
        block_output.reshape(rows3),
        input_grad.reshape(rows3),
        rest[0],
        rest[1],
        qkv_sum,
        proj_sum,
        rest[2],
        rest[3],
        up_sum,
        down_sum,
        rest[4],
        rest[5],
    )


def solution(mesh):
    placed = (
        P("batch", "seq", None),
        P("batch", "seq"),
        P(),
        P("batch", None),
        P("batch", "seq"),
        P(),
        P(),
        P(),
        P(),
        P(),
        P(),
        P("batch", None, None),
        P("batch", None, None),
        P("batch", "seq", None),
    )
    return jax.shard_map(
        local,
        mesh=mesh,
        in_specs=placed,
        out_specs=(
            P("batch", "seq", None),
            P("batch", "seq", None),
            P(),
            P(),
            P(),
            P(),
            P(),
            P(),
            P("batch", None, "seq"),
            P("batch", "seq", None),
            P(),
            P("batch", "seq", None),
        ),
        check_vma=False,
    )
```

profile of v0, /device:TPU:1, one launch (start us, length us, event | category | flops | bytes accessed | tf_op | source)
XLA Modules:
  0.0 298.4 jit_solution(9095489223228602481)
XLA Ops:
  7.2 5.3 %collective-permute-start = (bf16[4,128,768]{2,1,0:T(8,128)(2,1)}, bf16[4,128,768]{2,1,0:T(8,128)(2,1)}, u32[]{:S(2)}, u32[]{:S(2)}) collective-permute-start(bf16[4,128,768]{2,1,0:T(8,128)(2,1)} %x.3), channel_id=1, source_target_pairs={{0,2},{1,3},{2,4},{3,5},{4,6},{5,7},{8,10},{9,11},{10,12},{11,13},... | collective-permute-start | bytes 2359304 | tf_op jit(solution)/shard_map/ppermute | solution.py:621
  12.4 1.4 pad_bitcast_fusion.table
  13.8 0.6 pad_add_fusion.place
  14.4 3.7 %route.1 = (s32[8,512]{1,0:T(8,128)}, f32[16,128]{1,0:T(8,128)}, bf16[1024,768]{1,0:T(8,128)(2,1)}) custom-call(s32[2]{0:T(128)} %pad_add_fusion.place, s32[4,128]{1,0:T(4,128)} %tok.1, s32[64,128]{1,0:T(8,128)} %pad_bitcast_fusion.table, s32[4,128]{1,0:T(4,128)} %turn.5, bf16[512,768]{1,0:T(8,128)(2,1)} %bitcast.93), custom_call_target="tpu_custom_call" | custom-call | flops 1000000000 | bytes 2420744 | tf_op jit(solution)/shard_map/route/pallas_call | solution.py:39
  18.1 6.9 %all-to-all-start.1 = ((bf16[16,64,768]{2,1,0:T(8,128)(2,1)}), bf16[16,64,768]{2,1,0:T(8,128)(2,1)}, u32[]{:S(2)}, u32[]{:S(2)}) async-start(bf16[16,64,768]{2,1,0:T(8,128)(2,1)} %bitcast.70), calls=%async_computation.1 | async-start | bytes 3145728 | tf_op jit(solution)/shard_map/all_to_all | solution.py:604
  25.0 1.3 collective-permute-start.1
  26.3 5.8 %own.1 = (bf16[512,768]{1,0:T(8,128)(2,1)}, bf16[512,768]{1,0:T(8,128)(2,1)}, bf16[512,1536]{1,0:T(8,128)(2,1)}) custom-call(bf16[512,768]{1,0:T(8,128)(2,1)} %bitcast.59, f32[768]{0:T(1024)} %gain.7, f32[768]{0:T(1024)} %bias.5, bf16[768,2304]{1,0:T(8,128)(2,1)} %weight.7), custom_call_target="tpu_custom_call" | custom-call | flops 1800000000 | bytes 7477248 | tf_op jit(solution)/shard_map/own/pallas_call | solution.py:39
  32.1 4.9 %collective-permute-start.2 = (bf16[4,128,768]{2,1,0:T(8,128)(2,1)}, bf16[4,128,768]{2,1,0:T(8,128)(2,1)}, u32[]{:S(2)}, u32[]{:S(2)}) collective-permute-start(bf16[4,128,768]{2,1,0:T(8,128)(2,1)} %collective-permute-done.behind_two), channel_id=1, source_target_pairs={{1,0},{3,2},{5,4},{7,6},{9,8},{11,10},{13,12},{15,14},{17,16},{19,... | collective-permute-start | bytes 2359304 | tf_op jit(solution)/shard_map/ppermute | solution.py:640
  37.1 1.3 collective-permute-done.2.late
  38.4 15.7 %forward.1 = (bf16[4,256,768]{2,1,0:T(8,128)(2,1)}, bf16[4,384,1536]{2,1,0:T(8,128)(2,1)}, bf16[4,128,768]{2,1,0:T(8,128)(2,1)}, f32[4,8,256]{2,1,0:T(8,128)}, f...) custom-call(s32[2]{0:T(128)} %pad_add_fusion.place, s32[4,8]{1,0:T(4,128)} %lengths.3, f32[768]{0:T(1024)} %gain.7, ...), custom_call_target="tpu_custom_call" | custom-call | flops 1000000000 | bytes 20508808 | tf_op jit(solution)/shard_map/forward/pallas_call | solution.py:39
  54.1 7.2 %all-to-all-start = ((bf16[16,64,768]{2,1,0:T(8,128)(2,1)}), bf16[16,64,768]{2,1,0:T(8,128)(2,1)}, u32[]{:S(2)}, u32[]{:S(2)}) async-start(bf16[16,64,768]{2,1,0:T(8,128)(2,1)} %bitcast.71), calls=%async_computation | async-start | bytes 3145728 | tf_op jit(solution)/shard_map/all_to_all | solution.py:604
  61.3 3.8 %turn.4.turned = bf16[784,1536]{1,0:T(8,128)(2,1)} custom-call(bf16[512,768]{1,0:T(8,128)(2,1)} %get-tuple-element.62.unit, bf16[1024,768]{1,0:T(8,128)(2,1)} %bitcast.73), custom_call_target="tpu_custom_call" | custom-call | flops 1000000 | bytes 4767744 | tf_op jit(solution)/shard_map/turn/pallas_call | solution.py:39
  65.1 9.1 %active_grad.1.raw = bf16[4,1024,768]{2,1,0:T(8,128)(2,1)} custom-call(bf16[1024,768]{1,0:T(8,128)(2,1)} %bitcast.10.grad, bf16[3072,768]{1,0:T(8,128)(2,1)} %bitcast.91), custom_call_target="tpu_custom_call" | custom-call | flops 4800000000 | bytes 12582912 | tf_op jit(solution)/shard_map/active_grad/pallas_call | solution.py:39
  74.3 11.1 %all-to-all-done = bf16[16,64,768]{2,1,0:T(8,128)(2,1)} async-done(((bf16[16,64,768]{2,1,0:T(8,128)(2,1)}), bf16[16,64,768]{2,1,0:T(8,128)(2,1)}, u32[]{:S(2)}, u32[]{:S(2)}) %all-to-all-start) | async-done | bytes 1572896 | tf_op jit(solution)/shard_map/all_to_all | solution.py:604
  85.4 16.3 %expert.1 = (bf16[4,1024,768]{2,1,0:T(8,128)(2,1)}, bf16[4,1024,768]{2,1,0:T(8,128)(2,1)}, bf16[1024,768]{1,0:T(8,128)(2,1)}) custom-call(bf16[1024,768]{1,0:T(8,128)(2,1)} %bitcast.8.x, bf16[768,3072]{1,0:T(8,128)(2,1)} %bitcast.90, bf16[4,1024,768]{2,1,0:T(8,128)(2,1)} %active_grad.1.raw), custom_call_target="tpu_custom_call" | custom-call | flops 9699999744 | bytes 26738688 | tf_op jit(solution)/shard_map/expert/pallas_call | solution.py:39
  101.7 4.4 %all-to-all-start.3 = ((bf16[16,64,768]{2,1,0:T(8,128)(2,1)}), bf16[16,64,768]{2,1,0:T(8,128)(2,1)}, u32[]{:S(2)}, u32[]{:S(2)}) async-start(bf16[16,64,768]{2,1,0:T(8,128)(2,1)} %bitcast.72), calls=%async_computation.3 | async-start | bytes 3145728 | tf_op jit(solution)/shard_map/all_to_all | solution.py:604
  106.2 22.3 %weights.1 = (bf16[1024,768]{1,0:T(8,128)(2,1)}, bf16[8,1536,384]{2,1,0:T(8,128)(2,1)}) custom-call(bf16[1024,768]{1,0:T(8,128)(2,1)} %bitcast.8.x, bf16[1024,768]{1,0:T(8,128)(2,1)} %bitcast.10.grad, bf16[4,1024,768]{2,1,0:T(8,128)(2,1)} %get-tuple-element.65.active, bf16[4,1024,768]{2,1,0:T(8,128)(2,1)} %get-tuple-element.66.hidden_grad, ...), custom_call_target="tpu_custom_call" | custom-call | flops 14499999744 | bytes 31457280 | tf_op jit(solution)/shard_map/weights/pallas_call | solution.py:39
  128.5 6.6 %all-to-all-start.2 = ((bf16[16,64,768]{2,1,0:T(8,128)(2,1)}), bf16[16,64,768]{2,1,0:T(8,128)(2,1)}, u32[]{:S(2)}, u32[]{:S(2)}) async-start(bf16[16,64,768]{2,1,0:T(8,128)(2,1)} %bitcast.14), calls=%async_computation.2 | async-start | bytes 3145728 | tf_op jit(solution)/shard_map/all_to_all | solution.py:604
  135.1 36.6 %backward.1 = (f32[512,768]{1,0:T(8,128)}, bf16[512,768]{1,0:T(8,128)(2,1)}, bf16[512,1536]{1,0:T(8,128)(2,1)}, bf16[4,128,768]{2,1,0:T(8,128)(2,1)}, bf16[4,128...) custom-call(s32[2]{0:T(128)} %pad_add_fusion.place, s32[4,8]{1,0:T(4,128)} %lengths.3, ...), custom_call_target="tpu_custom_call" | custom-call | flops 16000000000 | bytes 28167304 | tf_op jit(solution)/shard_map/backward/pallas_call | solution.py:39
  171.7 2.4 collective-permute-start.5
  174.1 5.0 %collective-permute-done.5 = bf16[5120,256]{1,0:T(8,128)(2,1)S(1)} collective-permute-done((bf16[5120,256]{1,0:T(8,128)(2,1)}, bf16[5120,256]{1,0:T(8,128)(2,1)S(1)}, u32[]{:S(2)}, u32[]{:S(2)}) %collective-permute-start.5) | collective-permute-done | bytes 2621472 | tf_op jit(solution)/shard_map/ppermute | solution.py:741
  179.1 1.7 add_convert_fusion
  180.8 2.6 collective-permute-start.8
  183.4 8.5 %collective-permute-done.8 = bf16[1280,256]{1,0:T(8,128)(2,1)} collective-permute-done((bf16[1280,256]{1,0:T(8,128)(2,1)S(1)}, bf16[1280,256]{1,0:T(8,128)(2,1)}, u32[]{:S(2)}, u32[]{:S(2)}) %collective-permute-start.8) | collective-permute-done | bytes 655392 | tf_op jit(solution)/shard_map/ppermute | solution.py:556
  192.0 2.2 convert_add_fusion
  194.2 0.2 collective-permute-start.6
  194.4 1.5 collective-permute-start.3
  195.9 1.3 collective-permute-start.9
  197.2 6.8 %collective-permute-done.6 = bf16[1280,256]{1,0:T(8,128)(2,1)S(1)} collective-permute-done((bf16[1280,256]{1,0:T(8,128)(2,1)S(1)}, bf16[1280,256]{1,0:T(8,128)(2,1)S(1)}, u32[]{:S(2)}, u32[]{:S(2)}) %collective-permute-start.6) | collective-permute-done | bytes 655392 | tf_op jit(solution)/shard_map/ppermute | solution.py:556
  204.0 1.5 convert_add_fusion.1
  205.6 2.6 collective-permute-start.7
  208.2 0.1 add_select_fusion
  208.3 1.3 collective-permute-start.4
  209.7 3.4 %collective-permute-done.7 = bf16[640,256]{1,0:T(8,128)(2,1)S(1)} collective-permute-done((bf16[640,256]{1,0:T(8,128)(2,1)S(1)}, bf16[640,256]{1,0:T(8,128)(2,1)S(1)}, u32[]{:S(2)}, u32[]{:S(2)}) %collective-permute-start.7) | collective-permute-done | bytes 327712 | tf_op jit(solution)/shard_map/ppermute | solution.py:578
  213.2 2.3 collective-permute-start.10
  215.5 0.9 collective-permute-start.11
  216.4 1.8 collective-permute-start.12
  218.2 0.8 collective-permute-done.10
  219.0 1.9 collective-permute-done.11
  220.9 0.4 collective-permute-done.12
  221.4 5.6 %collective-permute-done.4 = bf16[4,128,768]{2,1,0:T(8,128)(2,1)} collective-permute-done((bf16[4,128,768]{2,1,0:T(8,128)(2,1)S(1)}, bf16[4,128,768]{2,1,0:T(8,128)(2,1)}, u32[]{:S(2)}, u32[]{:S(2)}) %collective-permute-start.4) | collective-permute-done | bytes 786464 | tf_op jit(solution)/shard_map/ppermute | solution.py:746
  227.0 2.7 collective-permute-start.13
  229.6 0.2 collective-permute-start.14
  229.8 2.7 collective-permute-start.15
  232.5 4.0 %output.1 = bf16[512,768]{1,0:T(8,128)(2,1)} custom-call(f32[512,768]{1,0:T(8,128)} %get-tuple-element.60.after, s32[8,512]{1,0:T(8,128)} %get-tuple-element.55.target, bf16[1024,768]{1,0:T(8,128)(2,1)} %bitcast.15.returned), custom_call_target="tpu_custom_call" | custom-call | flops 800000000 | bytes 3948544 | tf_op jit(solution)/shard_map/output/pallas_call | solution.py:39
  236.7 2.9 expert_sum.1
  239.6 3.5 %collective-permute-start.16 = (bf16[2,160,256]{2,1,0:T(8,128)(2,1)S(1)}, bf16[2,160,256]{2,1,0:T(8,128)(2,1)S(1)}, u32[]{:S(2)}, u32[]{:S(2)}) collective-permute-start(bf16[2,160,256]{2,1,0:T(8,128)(2,1)S(1)} %add_convert_fusion.4), channel_id=1, source_target_pairs={{0,32},{1,9},{2,34},{3,11},{4,36},{5,13},{6,38},{7,15},{8,40},{9,1... | collective-permute-start | bytes 491528 | tf_op jit(solution)/shard_map/ppermute | solution.py:590
  243.1 3.4 %collective-permute-start.17 = (bf16[2,160,256]{2,1,0:T(8,128)(2,1)S(1)}, bf16[2,160,256]{2,1,0:T(8,128)(2,1)S(1)}, u32[]{:S(2)}, u32[]{:S(2)}) collective-permute-start(bf16[2,160,256]{2,1,0:T(8,128)(2,1)S(1)} %add_convert_fusion.4), channel_id=1, source_target_pairs={{0,64},{1,17},{2,66},{3,19},{4,68},{5,21},{6,70},{7,23},{8,72},{9,... | collective-permute-start | bytes 491528 | tf_op jit(solution)/shard_map/ppermute | solution.py:590
  246.5 1.2 collective-permute-start.18
  247.7 0.6 collective-permute-done.16
  248.3 2.9 collective-permute-done.17
  251.8 7.8 %input_grad.1 = f32[512,768]{1,0:T(8,128)} custom-call(f32[1]{0:T(128)} %bitcast.17.even, f32[768]{0:T(1024)} %gain.7, bf16[512,768]{1,0:T(8,128)(2,1)} %get-tuple-element.73.query_grad, bf16[512,1536]{1,0:T(8,128)(2,1)} %get-tuple-element.74.own_grad, bf16[768,2304]{1,0:T(8,128)(2,1)} %weight.7, bf16[512,768]{1,0:T(8,128)(2,1)} %bitcast.60, ...), custom_call_target="tpu_custom_call" | custom-call | flops 3000000000 | bytes 11406340 | tf_op jit(solution)/shard_map/input_grad/pallas_call | solution.py:39
  259.6 1.2 maximum_select_fusion.2
  260.8 1.5 collective-permute-start.20
  262.4 2.6 collective-permute-start.22
  265.0 5.5 %collective-permute-done.20 = bf16[1280,256]{1,0:T(8,128)(2,1)S(1)} collective-permute-done((bf16[1280,256]{1,0:T(8,128)(2,1)S(1)}, bf16[1280,256]{1,0:T(8,128)(2,1)S(1)}, u32[]{:S(2)}, u32[]{:S(2)}) %collective-permute-start.20) | collective-permute-done | bytes 655392 | tf_op jit(solution)/shard_map/ppermute | solution.py:566
  270.6 0.2 maximum_select_fusion
  270.8 2.6 collective-permute-done.22
  273.4 0.2 maximum_select_fusion.1
  273.6 1.7 pad_maximum_fusion.mine
  275.3 6.1 %collective-permute-start.23 = (bf16[5120,256]{1,0:T(8,128)(2,1)}, bf16[5120,256]{1,0:T(8,128)(2,1)}, u32[]{:S(2)}, u32[]{:S(2)}) collective-permute-start(bf16[5120,256]{1,0:T(8,128)(2,1)} %pad_maximum_fusion.mine), channel_id=1, source_target_pairs={{0,1},{1,0},{2,3},{3,2},{4,5},{5,4},{6,7},{7,6},{8,9},{9,8},{10,11... | collective-permute-start | bytes 7864328 | tf_op jit(solution)/shard_map/ppermute | solution.py:771
  281.4 0.7 slice.22.tail
  282.1 4.3 %finish_mine.1 = (f32[768,2304]{1,0:T(8,128)}, f32[768,768]{1,0:T(8,128)}) custom-call(s32[2]{0:T(128)} %pad_add_fusion.place, bf16[5120,256]{1,0:T(8,128)(2,1)} %pad_maximum_fusion.mine), custom_call_target="tpu_custom_call" | custom-call | flops 1000000 | bytes 12058632 | tf_op jit(solution)/shard_map/finish_mine/pallas_call | solution.py:39
  286.4 4.9 %finish_other.1 = (f32[768,2304]{1,0:T(8,128)}, f32[768,768]{1,0:T(8,128)}, f32[768]{0:T(1024)}, f32[768]{0:T(1024)}, f32[768]{0:T(1024)}, /*index=5*/f32[768]{0:T(1024)}, s32[16]{0:T(128)}, s32[1,1,16]{2,1,0:T(1,128)}) custom-call(s32[2]{0:T(128)} %pad_add_fusion.place, ...), custom_call_target="tpu_custom_call", output_to_operand_aliasing={{0}: (3, {}), {1}: (4, {})} | custom-call | flops 1000000 | bytes 21770376 | tf_op jit(solution)/shard_map/finish_other/pallas_call | solution.py:39
  (39 shorter events, 1.2 us)
Async XLA Ops:
  7.2 25.0 %collective-permute-start = (bf16[4,128,768]{2,1,0:T(8,128)(2,1)}, bf16[4,128,768]{2,1,0:T(8,128)(2,1)}, u32[]{:S(2)}, u32[]{:S(2)}) collective-permute-start(bf16[4,128,768]{2,1,0:T(8,128)(2,1)} %x.3), channel_id=1, source_target_pairs={{0,2},{1,3},{2,4},{3,5},{4,6},{5,7},{8,10},{9,11},{10,12},{11,13},... | collective-permute-start | bytes 2359304 | tf_op jit(solution)/shard_map/ppermute | solution.py:621
  18.1 6.9 %copy-start = (bf16[4,128,768]{2,1,0:T(8,128)(2,1)S(1)}, bf16[4,128,768]{2,1,0:T(8,128)(2,1)}, u32[]{:S(2)}) copy-start(bf16[4,128,768]{2,1,0:T(8,128)(2,1)} %x.3) | copy-start | bytes 2359300
  18.1 36.0 %all-to-all-start.1 = ((bf16[16,64,768]{2,1,0:T(8,128)(2,1)}), bf16[16,64,768]{2,1,0:T(8,128)(2,1)}, u32[]{:S(2)}, u32[]{:S(2)}) async-start(bf16[16,64,768]{2,1,0:T(8,128)(2,1)} %bitcast.70), calls=%async_computation.1 | async-start | bytes 3145728 | tf_op jit(solution)/shard_map/all_to_all | solution.py:604
  25.0 12.0 %collective-permute-start.1 = (bf16[4,128,768]{2,1,0:T(8,128)(2,1)S(1)}, bf16[4,128,768]{2,1,0:T(8,128)(2,1)}, u32[]{:S(2)}, u32[]{:S(2)}) collective-permute-start(bf16[4,128,768]{2,1,0:T(8,128)(2,1)S(1)} %copy-done), channel_id=1, source_target_pairs={{0,1},{2,3},{4,5},{6,7},{8,9},{10,11},{12,13},{14,15},{16,17},{18,... | collective-permute-start | bytes 2359304 | tf_op jit(solution)/shard_map/ppermute | solution.py:622
  32.1 6.3 %collective-permute-start.2 = (bf16[4,128,768]{2,1,0:T(8,128)(2,1)}, bf16[4,128,768]{2,1,0:T(8,128)(2,1)}, u32[]{:S(2)}, u32[]{:S(2)}) collective-permute-start(bf16[4,128,768]{2,1,0:T(8,128)(2,1)} %collective-permute-done.behind_two), channel_id=1, source_target_pairs={{1,0},{3,2},{5,4},{7,6},{9,8},{11,10},{13,12},{15,14},{17,16},{19,... | collective-permute-start | bytes 2359304 | tf_op jit(solution)/shard_map/ppermute | solution.py:640
  54.1 31.2 %all-to-all-start = ((bf16[16,64,768]{2,1,0:T(8,128)(2,1)}), bf16[16,64,768]{2,1,0:T(8,128)(2,1)}, u32[]{:S(2)}, u32[]{:S(2)}) async-start(bf16[16,64,768]{2,1,0:T(8,128)(2,1)} %bitcast.71), calls=%async_computation | async-start | bytes 3145728 | tf_op jit(solution)/shard_map/all_to_all | solution.py:604
  101.7 26.8 %all-to-all-start.3 = ((bf16[16,64,768]{2,1,0:T(8,128)(2,1)}), bf16[16,64,768]{2,1,0:T(8,128)(2,1)}, u32[]{:S(2)}, u32[]{:S(2)}) async-start(bf16[16,64,768]{2,1,0:T(8,128)(2,1)} %bitcast.72), calls=%async_computation.3 | async-start | bytes 3145728 | tf_op jit(solution)/shard_map/all_to_all | solution.py:604
  106.1 130.5 %reduce-scatter.2.cloned.1.call-start = ((), (), s32[]{:S(2)}) async-start(), calls=%async_computation.5 | async-start | bytes 10616832 | tf_op jit(solution)/shard_map/reduce_scatter | solution.py:714
  128.5 43.2 %all-to-all-start.2 = ((bf16[16,64,768]{2,1,0:T(8,128)(2,1)}), bf16[16,64,768]{2,1,0:T(8,128)(2,1)}, u32[]{:S(2)}, u32[]{:S(2)}) async-start(bf16[16,64,768]{2,1,0:T(8,128)(2,1)} %bitcast.14), calls=%async_computation.2 | async-start | bytes 3145728 | tf_op jit(solution)/shard_map/all_to_all | solution.py:604
  171.7 7.4 %collective-permute-start.5 = (bf16[5120,256]{1,0:T(8,128)(2,1)}, bf16[5120,256]{1,0:T(8,128)(2,1)S(1)}, u32[]{:S(2)}, u32[]{:S(2)}) collective-permute-start(bf16[5120,256]{1,0:T(8,128)(2,1)} %get-tuple-element.80), channel_id=1, source_target_pairs={{0,1},{1,0},{2,3},{3,2},{4,5},{5,4},{6,7},{7,6},{8,9},{9,8},{10,11... | collective-permute-start | bytes 7864328 | tf_op jit(solution)/shard_map/ppermute | solution.py:741
  179.1 4.4 %copy-start.2 = (bf16[5120,256]{1,0:T(8,128)(2,1)}, bf16[5120,256]{1,0:T(8,128)(2,1)S(1)}, u32[]{:S(2)}) copy-start(bf16[5120,256]{1,0:T(8,128)(2,1)S(1)} %collective-permute-done.5) | copy-start | bytes 7864324
  180.8 11.1 %collective-permute-start.8 = (bf16[1280,256]{1,0:T(8,128)(2,1)S(1)}, bf16[1280,256]{1,0:T(8,128)(2,1)}, u32[]{:S(2)}, u32[]{:S(2)}) collective-permute-start(bf16[1280,256]{1,0:T(8,128)(2,1)S(1)} %add_convert_fusion), channel_id=1, source_target_pairs={{0,24},{1,97},{2,26},{3,99},{4,28},{5,101},{6,30},{7,103},{8,16},{... | collective-permute-start | bytes 1966088 | tf_op jit(solution)/shard_map/ppermute | solution.py:556
  194.2 9.8 %collective-permute-start.6 = (bf16[1280,256]{1,0:T(8,128)(2,1)S(1)}, bf16[1280,256]{1,0:T(8,128)(2,1)S(1)}, u32[]{:S(2)}, u32[]{:S(2)}) collective-permute-start(bf16[1280,256]{1,0:T(8,128)(2,1)S(1)} %get-tuple-element.99), channel_id=1, source_target_pairs={{0,8},{1,33},{2,10},{3,35},{4,12},{5,37},{6,14},{7,39},{8,0},{9,41... | collective-permute-start | bytes 1966088 | tf_op jit(solution)/shard_map/ppermute | solution.py:556
  194.4 13.8 %collective-permute-start.3 = (bf16[4,128,768]{2,1,0:T(8,128)(2,1)}, bf16[4,128,768]{2,1,0:T(8,128)(2,1)S(1)}, u32[]{:S(2)}, u32[]{:S(2)}) collective-permute-start(bf16[4,128,768]{2,1,0:T(8,128)(2,1)} %get-tuple-element.75), channel_id=1, source_target_pairs={{0,1},{1,0},{2,3},{3,2},{4,5},{5,4},{6,7},{7,6},{8,9},{9,8},{10,11... | collective-permute-start | bytes 2359304 | tf_op jit(solution)/shard_map/ppermute | solution.py:744
  195.9 12.3 %copy-start.3 = (bf16[4,128,768]{2,1,0:T(8,128)(2,1)S(1)}, bf16[4,128,768]{2,1,0:T(8,128)(2,1)}, u32[]{:S(2)}) copy-start(bf16[4,128,768]{2,1,0:T(8,128)(2,1)} %get-tuple-element.76) | copy-start | bytes 2359300
  195.9 13.7 %collective-permute-start.9 = (bf16[640,256]{1,0:T(8,128)(2,1)S(1)}, bf16[640,256]{1,0:T(8,128)(2,1)S(1)}, u32[]{:S(2)}, u32[]{:S(2)}) collective-permute-start(bf16[640,256]{1,0:T(8,128)(2,1)S(1)} %dynamic-slice_convert_fusion), channel_id=1, source_target_pairs={{0,8},{1,33},{2,10},{3,35},{4,12},{5,37},{6,14},{7,39},{8,0},{9,41... | collective-permute-start | bytes 983048 | tf_op jit(solution)/shard_map/ppermute | solution.py:578
  205.6 7.5 %collective-permute-start.7 = (bf16[640,256]{1,0:T(8,128)(2,1)S(1)}, bf16[640,256]{1,0:T(8,128)(2,1)S(1)}, u32[]{:S(2)}, u32[]{:S(2)}) collective-permute-start(bf16[640,256]{1,0:T(8,128)(2,1)S(1)} %dynamic-slice_convert_fusion.1), channel_id=1, source_target_pairs={{0,24},{1,97},{2,26},{3,99},{4,28},{5,101},{6,30},{7,103},{8,16},{... | collective-permute-start | bytes 983048 | tf_op jit(solution)/shard_map/ppermute | solution.py:578
  208.2 1.5 copy-start.1
  208.3 18.7 %collective-permute-start.4 = (bf16[4,128,768]{2,1,0:T(8,128)(2,1)S(1)}, bf16[4,128,768]{2,1,0:T(8,128)(2,1)}, u32[]{:S(2)}, u32[]{:S(2)}) collective-permute-start(bf16[4,128,768]{2,1,0:T(8,128)(2,1)S(1)} %add_select_fusion), channel_id=1, source_target_pairs={{2,0},{3,1},{4,2},{5,3},{6,4},{7,5},{10,8},{11,9},{12,10},{13,11},... | collective-permute-start | bytes 2359304 | tf_op jit(solution)/shard_map/ppermute | solution.py:746
  213.2 5.8 %collective-permute-start.10 = (bf16[2,160,256]{2,1,0:T(8,128)(2,1)S(1)}, bf16[2,160,256]{2,1,0:T(8,128)(2,1)S(1)}, u32[]{:S(2)}, u32[]{:S(2)}) collective-permute-start(bf16[2,160,256]{2,1,0:T(8,128)(2,1)S(1)} %get-tuple-element.106), channel_id=1, source_target_pairs={{0,64},{1,17},{2,66},{3,19},{4,68},{5,21},{6,70},{7,23},{8,72},{9,... | collective-permute-start | bytes 491528 | tf_op jit(solution)/shard_map/ppermute | solution.py:584
  215.5 5.4 %collective-permute-start.11 = (bf16[2,160,256]{2,1,0:T(8,128)(2,1)S(1)}, bf16[2,160,256]{2,1,0:T(8,128)(2,1)S(1)}, u32[]{:S(2)}, u32[]{:S(2)}) collective-permute-start(bf16[2,160,256]{2,1,0:T(8,128)(2,1)S(1)} %get-tuple-element.107), channel_id=1, source_target_pairs={{0,32},{1,9},{2,34},{3,11},{4,36},{5,13},{6,38},{7,15},{8,40},{9,1... | collective-permute-start | bytes 491528 | tf_op jit(solution)/shard_map/ppermute | solution.py:584
  216.4 4.9 %collective-permute-start.12 = (bf16[2,160,256]{2,1,0:T(8,128)(2,1)S(1)}, bf16[2,160,256]{2,1,0:T(8,128)(2,1)S(1)}, u32[]{:S(2)}, u32[]{:S(2)}) collective-permute-start(bf16[2,160,256]{2,1,0:T(8,128)(2,1)S(1)} %get-tuple-element.108), channel_id=1, source_target_pairs={{0,96},{1,25},{2,98},{3,27},{4,100},{5,29},{6,102},{7,31},{8,104},... | collective-permute-start | bytes 491528 | tf_op jit(solution)/shard_map/ppermute | solution.py:584
  227.0 9.6 %collective-permute-start.13 = (bf16[2,160,256]{2,1,0:T(8,128)(2,1)S(1)}, bf16[2,160,256]{2,1,0:T(8,128)(2,1)S(1)}, u32[]{:S(2)}, u32[]{:S(2)}) collective-permute-start(bf16[2,160,256]{2,1,0:T(8,128)(2,1)S(1)} %fusion.2), channel_id=1, source_target_pairs={{0,4},{1,5},{2,6},{3,7},{4,0},{5,1},{6,2},{7,3},{8,12},{9,13},{10,... | collective-permute-start | bytes 491528 | tf_op jit(solution)/shard_map/ppermute | solution.py:588
  229.6 6.9 %collective-permute-start.14 = (bf16[2,160,256]{2,1,0:T(8,128)(2,1)S(1)}, bf16[2,160,256]{2,1,0:T(8,128)(2,1)S(1)}, u32[]{:S(2)}, u32[]{:S(2)}) collective-permute-start(bf16[2,160,256]{2,1,0:T(8,128)(2,1)S(1)} %fusion.2), channel_id=1, source_target_pairs={{0,2},{1,3},{2,4},{3,5},{4,6},{5,7},{6,0},{7,1},{8,10},{9,11},{10,... | collective-permute-start | bytes 491528 | tf_op jit(solution)/shard_map/ppermute | solution.py:588
  229.8 6.7 %collective-permute-start.15 = (bf16[2,160,256]{2,1,0:T(8,128)(2,1)S(1)}, bf16[2,160,256]{2,1,0:T(8,128)(2,1)S(1)}, u32[]{:S(2)}, u32[]{:S(2)}) collective-permute-start(bf16[2,160,256]{2,1,0:T(8,128)(2,1)S(1)} %fusion.2), channel_id=1, source_target_pairs={{0,6},{1,7},{2,0},{3,1},{4,2},{5,3},{6,4},{7,5},{8,14},{9,15},{10,... | collective-permute-start | bytes 491528 | tf_op jit(solution)/shard_map/ppermute | solution.py:588
  239.6 8.7 %collective-permute-start.16 = (bf16[2,160,256]{2,1,0:T(8,128)(2,1)S(1)}, bf16[2,160,256]{2,1,0:T(8,128)(2,1)S(1)}, u32[]{:S(2)}, u32[]{:S(2)}) collective-permute-start(bf16[2,160,256]{2,1,0:T(8,128)(2,1)S(1)} %add_convert_fusion.4), channel_id=1, source_target_pairs={{0,32},{1,9},{2,34},{3,11},{4,36},{5,13},{6,38},{7,15},{8,40},{9,1... | collective-permute-start | bytes 491528 | tf_op jit(solution)/shard_map/ppermute | solution.py:590
  243.1 8.1 %collective-permute-start.17 = (bf16[2,160,256]{2,1,0:T(8,128)(2,1)S(1)}, bf16[2,160,256]{2,1,0:T(8,128)(2,1)S(1)}, u32[]{:S(2)}, u32[]{:S(2)}) collective-permute-start(bf16[2,160,256]{2,1,0:T(8,128)(2,1)S(1)} %add_convert_fusion.4), channel_id=1, source_target_pairs={{0,64},{1,17},{2,66},{3,19},{4,68},{5,21},{6,70},{7,23},{8,72},{9,... | collective-permute-start | bytes 491528 | tf_op jit(solution)/shard_map/ppermute | solution.py:590
  246.5 4.8 %collective-permute-start.18 = (bf16[2,160,256]{2,1,0:T(8,128)(2,1)S(1)}, bf16[2,160,256]{2,1,0:T(8,128)(2,1)S(1)}, u32[]{:S(2)}, u32[]{:S(2)}) collective-permute-start(bf16[2,160,256]{2,1,0:T(8,128)(2,1)S(1)} %add_convert_fusion.4), channel_id=1, source_target_pairs={{0,96},{1,25},{2,98},{3,27},{4,100},{5,29},{6,102},{7,31},{8,104},... | collective-permute-start | bytes 491528 | tf_op jit(solution)/shard_map/ppermute | solution.py:590
  251.6 8.0 %collective-permute-start.19 = (bf16[640,256]{1,0:T(8,128)(2,1)S(1)}, bf16[640,256]{1,0:T(8,128)(2,1)}, u32[]{:S(2)}, u32[]{:S(2)}) collective-permute-start(bf16[640,256]{1,0:T(8,128)(2,1)S(1)} %bitcast.78), channel_id=1, source_target_pairs={{0,24},{1,97},{2,26},{3,99},{4,28},{5,101},{6,30},{7,103},{8,16},{... | collective-permute-start | bytes 983048 | tf_op jit(solution)/shard_map/ppermute | solution.py:566
  251.7 10.6 %collective-permute-start.21 = (bf16[640,256]{1,0:T(8,128)(2,1)S(1)}, bf16[640,256]{1,0:T(8,128)(2,1)S(1)}, u32[]{:S(2)}, u32[]{:S(2)}) collective-permute-start(bf16[640,256]{1,0:T(8,128)(2,1)S(1)} %bitcast.76), channel_id=1, source_target_pairs={{0,8},{1,33},{2,10},{3,35},{4,12},{5,37},{6,14},{7,39},{8,0},{9,41... | collective-permute-start | bytes 983048 | tf_op jit(solution)/shard_map/ppermute | solution.py:566
  260.8 9.8 %collective-permute-start.20 = (bf16[1280,256]{1,0:T(8,128)(2,1)S(1)}, bf16[1280,256]{1,0:T(8,128)(2,1)S(1)}, u32[]{:S(2)}, u32[]{:S(2)}) collective-permute-start(bf16[1280,256]{1,0:T(8,128)(2,1)S(1)} %bitcast.66), channel_id=1, source_target_pairs={{0,8},{1,33},{2,10},{3,35},{4,12},{5,37},{6,14},{7,39},{8,0},{9,41... | collective-permute-start | bytes 1966088 | tf_op jit(solution)/shard_map/ppermute | solution.py:566
  262.4 11.0 %collective-permute-start.22 = (bf16[1280,256]{1,0:T(8,128)(2,1)S(1)}, bf16[1280,256]{1,0:T(8,128)(2,1)S(1)}, u32[]{:S(2)}, u32[]{:S(2)}) collective-permute-start(bf16[1280,256]{1,0:T(8,128)(2,1)S(1)} %bitcast.68), channel_id=1, source_target_pairs={{0,24},{1,97},{2,26},{3,99},{4,28},{5,101},{6,30},{7,103},{8,16},{... | collective-permute-start | bytes 1966088 | tf_op jit(solution)/shard_map/ppermute | solution.py:566
  275.3 11.1 %collective-permute-start.23 = (bf16[5120,256]{1,0:T(8,128)(2,1)}, bf16[5120,256]{1,0:T(8,128)(2,1)}, u32[]{:S(2)}, u32[]{:S(2)}) collective-permute-start(bf16[5120,256]{1,0:T(8,128)(2,1)} %pad_maximum_fusion.mine), channel_id=1, source_target_pairs={{0,1},{1,0},{2,3},{3,2},{4,5},{5,4},{6,7},{7,6},{8,9},{9,8},{10,11... | collective-permute-start | bytes 7864328 | tf_op jit(solution)/shard_map/ppermute | solution.py:771
Sparse Core Ops, SparseCore 0:
  128.6 59.1 reduce-scatter.1
where the time goes:
time: 302 us; the launch traced here: 298 us
  Pallas kernels  137 us (45%)
  starting transfers between devices  77.6 us (26%)
  waiting for transfers between devices  56.5 us (19%)
  between operations  14.6 us (5%)
  other arithmetic  10.1 us (3%)
    pallas_call x13, Pallas kernels, kernel_call(): pl.pallas_call(body, out_shape=outs, in_specs=in_specs or [VM] * len(args...  137 us
    all_to_all x4, starting transfers between devices, exchange(): lax.all_to_all(array.reshape(16, CAP, 768), 'batch', split_axis=0, concat...  25.1 us
    ppermute x2, waiting for transfers between devices, sum_start(): lax.ppermute(part(i, 1 - bits[i]).astype(BF), BOTH, first_pairs(PAIRS_OF[...  15.3 us
    all_to_all x4, waiting for transfers between devices, exchange(): lax.all_to_all(array.reshape(16, CAP, 768), 'batch', split_axis=0, concat...  11.1 us
    ppermute x4, waiting for transfers between devices, pair_gather(): lax.ppermute(data, BOTH, first_pairs(pair))  8.16 us
    ppermute x3, starting transfers between devices, sum_finish(): lax.ppermute(piece, BOTH, second_step(d))  8.1 us
    ppermute x1, starting transfers between devices, local(): other = lax.ppermute(mine, 'seq', SWAP)  6.07 us
  transfers between devices with their start and end apart: 29, of which 14 were waited for; matrix products, arithmetic and copies ran while one was open for 3% of the time, Pallas kernels for 38%

commit v1 on v0

--- a/solution.py
+++ b/solution.py
@@ -19,7 +19,8 @@
 DOWN_ONE = [(i + 1, i) for i in range(0, 8, 2)]
 AHEAD_TWO = [(i, i + 2) for i in range(6)]
 BACK_TWO = [(i + 2, i) for i in range(6)]
-HALF_ROWS = 5120
+HALF_ROWS = 4864
+PIECE = HALF_ROWS // 4
 VMEM_BYTES = 63 * 1024 * 1024
 GEMM_ROWS = 4608
 VM = pl.BlockSpec(memory_space=pltpu.VMEM)
@@ -440,48 +441,56 @@
     pltpu.make_async_copy(out.at[1], away, out_sems.at[6]).wait()
 
 
-def place_half(half, data, qkv, proj, stage, sems):
+def place_half(half, bits, pieces, qkv, proj, whole, stage, in_sems, sems):
+    loads = []
+    for i in range(2):
+        for j in range(2):
+            first = pl.multiple_of((2 * i + (bits[i] + j) % 2) * PIECE, PIECE)
+            target = whole.at[pl.ds(first, PIECE)]
+            loads.append(pltpu.make_async_copy(pieces[2 * i + j], target, in_sems.at[2 * i + j]))
+            loads[-1].start()
+    for copy in loads:
+        copy.wait()
     for j in range(6):
         lanes = slice(256 * (j % 3), 256 * (j % 3 + 1))
-        stage[j // 3, :, lanes] = data[768 * j : 768 * (j + 1), :].astype(F32)
+        stage[j // 3, :, lanes] = whole[768 * j : 768 * (j + 1), :].astype(F32)
+
+    def send(targets):
+        moves = [pltpu.make_async_copy(stage.at[i], target, sems.at[i]) for i, target in enumerate(targets)]
+        for copy in moves:
+            copy.start()
+        for copy in moves:
+            copy.wait()
 
     @pl.when(half == 0)
     def _():
-        one = pltpu.make_async_copy(stage.at[0], qkv.at[:, 0:768], sems.at[0])
-        two = pltpu.make_async_copy(stage.at[1], qkv.at[:, 768:1536], sems.at[1])
-        one.start()
-        two.start()
-        one.wait()
-        two.wait()
+        send([qkv.at[:, 0:768], qkv.at[:, 768:1536]])
 
     @pl.when(half == 1)
     def _():
-        one = pltpu.make_async_copy(stage.at[0], qkv.at[:, 1536:2304], sems.at[0])
-        two = pltpu.make_async_copy(stage.at[1], proj, sems.at[1])
-        one.start()
-        two.start()
-        one.wait()
-        two.wait()
-
-
-def finish_mine_kernel(place, mine, qkv, proj, stage, sems):
-    place_half(place[0] % 2, mine, qkv, proj, stage, sems)
+        send([qkv.at[:, 1536:2304], proj])
+
+
+def finish_mine_kernel(place, a, b, c, d, qkv, proj, tail, whole, stage, in_sems, sems):
+    place_half(place[0], (place[2], place[3]), (a, b, c, d), qkv, proj, whole, stage, in_sems, sems)
+    tail[...] = whole[GEMM_ROWS : GEMM_ROWS + 64, :]
 
 
 def finish_other_kernel(
-    place, other, tail, qkv_in, proj_in, qkv, proj, gain_one, bias_one, gain_two, bias_two, counts, received, stage, sems
+    place, tail, a, b, c, d, qkv_in, proj_in, qkv, proj, gain_one, bias_one, gain_two, bias_two, counts, received,
+    whole, stage, in_sems, sems,
 ):
-    both = tail[...].astype(F32) + other[GEMM_ROWS:, :].astype(F32)
+    place_half(1 - place[0], (place[4], place[5]), (a, b, c, d), qkv, proj, whole, stage, in_sems, sems)
+    both = tail[...].astype(F32) + whole[GEMM_ROWS : GEMM_ROWS + 64, :].astype(F32)
     for i, out in enumerate([gain_one, bias_one, gain_two, bias_two]):
         line = jnp.concatenate([both[16 * t + i : 16 * t + i + 1, :] for t in range(3)], axis=1)
         out[...] = line.reshape(768)
     every = both[48:64, 0:128]
     counts[...] = nt(jnp.ones((8, 128), BF), every.astype(BF))[0:1, :].astype(I32).reshape(16)
-    chosen = (iota((16, 128), 0) == place[1]) & ((iota((16, 128), 1) >> 4) == place[0])
+    chosen = (iota((16, 128), 0) == place[1]) & ((iota((16, 128), 1) >> 4) == place[6])
     mine = jnp.where(chosen, every, 0.0).astype(BF)
     fold = ((iota((128, 16), 0) & 15) == iota((128, 16), 1)).astype(F32).astype(BF)
     received[0] = jnp.sum(nn(mine, fold), axis=0, keepdims=True).astype(I32)
-    place_half(1 - place[0] % 2, other, qkv, proj, stage, sems)
 
 
 def expert_sum_kernel(parts, up, down):
@@ -541,16 +550,19 @@
     return lax.dynamic_index_in_dim(array, index % 4, 1, keepdims=False)
 
 
+def bits_of(place):
+    return [(place & 1) ^ (place >> 1), place >> 1]
+
+
 def sum_start(keep, got):
     seq, place = lax.axis_index("seq"), lax.axis_index("batch")
     core, x, y = seq % 2, place % 4, place // 4
     one, two = jnp.where(core == 0, x, y), jnp.where(core == 0, y, x)
-    bits = [(one & 1) ^ (one >> 1), one >> 1]
-    size = HALF_ROWS // 4
+    bits = bits_of(one)
 
     def part(stream, bit):
-        at = (stream * 2 + bit) * size
-        return rows_at(keep, at, size).astype(F32) + rows_at(got, at, size).astype(F32)
+        at = (stream * 2 + bit) * PIECE
+        return rows_at(keep, at, PIECE).astype(F32) + rows_at(got, at, PIECE).astype(F32)
 
     moved = [
         lax.ppermute(part(i, 1 - bits[i]).astype(BF), BOTH, first_pairs(PAIRS_OF[i])) for i in range(2)
@@ -571,29 +583,33 @@
 
 
 def sum_finish(bits, place, part, moved, beside):
-    size = HALF_ROWS // 8
+    size = PIECE // 2
+    moved = [after_all(moved[0], *beside[0]), moved[1]]
     sums = [part(i, bits[i]) + moved[i].astype(F32) for i in range(2)]
     sent = [rows_at(sums[i], (1 - bits[1 - i]) * size, size).astype(BF) for i in range(2)]
     stay = [rows_at(sums[i], bits[1 - i] * size, size) for i in range(2)]
     moved = [lax.ppermute(sent[i], BOTH, first_pairs(PAIRS_OF[1 - i])) for i in range(2)]
     chunks = [(a + b.astype(F32)).astype(BF) for a, b in zip(stay, moved)]
+    chunks[0] = after_all(chunks[0], *beside[1])
     size, lanes = chunks[0].shape
     grouped = jnp.stack(chunks).reshape(2, 4, size // 4, lanes)
     total = part_of(grouped, place).astype(F32)
     for d in (2, 1, 3):
         total = total + lax.ppermute(part_of(grouped, place + d), BOTH, second_step(d)).astype(F32)
-    whole = after_all(total.astype(BF), *beside[0])
+    whole = total.astype(BF)
     total = whole.astype(F32)
     for d in (2, 1, 3):
         total = total + lax.ppermute(whole, "seq", along_z(d)).astype(F32)
-    piece = after_all(total.astype(BF), *beside[1])
+    piece = total.astype(BF)
     parts = [piece] + [lax.ppermute(piece, BOTH, second_step(d)) for d in (1, 2, 3)]
     stack = jnp.stack(parts, axis=1)
     ordered = jnp.stack([part_of(stack, place - p + 4) for p in range(4)], axis=1).reshape(2, size, lanes)
     chunks = pair_gather([ordered[0], ordered[1]], bits[::-1], PAIRS_OF[::-1])
-    chunks[0] = after_all(chunks[0], *beside[2])
-    chunks = pair_gather(chunks, bits, PAIRS_OF)
-    return jnp.concatenate(chunks, axis=0)
+    moved = [lax.ppermute(data, BOTH, first_pairs(pair)) for pair, data in zip(PAIRS_OF, chunks)]
+    mine = [chunks[0], moved[0], chunks[1], moved[1]]
+    late = [after_all(a, *beside[2]) for a in moved]
+    swapped = [lax.ppermute(a, "seq", SWAP) for a in (chunks[0], late[0], chunks[1], late[1])]
+    return mine, swapped
 
 
 def after_all(value, *others):
@@ -739,9 +755,9 @@
         ],
     )
     got = lax.ppermute(after_all(away, returned), "seq", SWAP)
-    bits, turn, part, streams = sum_start(keep, got)
-
     from_one = lax.ppermute(input_one, "seq", SWAP)
+    bits, turn, part, streams = sum_start(keep, after_all(got, from_one))
+
     passed = jnp.where(odd == 1, input_two + from_one, input_two)
     from_two = lax.ppermute(passed, "seq", BACK_TWO)
     even = (1 - odd).astype(F32).reshape(1)
@@ -767,23 +783,27 @@
         [shape((1, 768, 384), F32), shape((1, 384, 768), F32)],
         [parts_sum], "expert_sum", 10**6,
     )
-    mine = sum_finish(bits, turn, part, streams, ([from_two], [block_output, up_sum], [input_grad]))
-    other = lax.ppermute(mine, "seq", SWAP)
+    mine, swapped = sum_finish(
+        bits, turn, part, streams, ([block_output, passed], [from_two, up_sum], [input_grad])
+    )
+    spots = jnp.stack([odd, owner, *bits, *bits_of(turn), seq]).astype(I32)
     sums = [shape((768, 2304), F32), shape((768, 768), F32)]
-    away_spec = [pl.BlockSpec(memory_space=pl.ANY)] * 2
-    landing = [pltpu.VMEM((2, 768, 768), F32), pltpu.SemaphoreType.DMA((2,))]
-    qkv_half, proj_half = kernel_call(
-        finish_mine_kernel, sums, [place, mine], "finish_mine", 10**6,
-        in_specs=[SM, VM], out_specs=away_spec, scratch=landing,
+    landing = [
+        pltpu.VMEM((HALF_ROWS, 256), BF), pltpu.VMEM((2, 768, 768), F32),
+        pltpu.SemaphoreType.DMA((4,)), pltpu.SemaphoreType.DMA((2,)),
+    ]
+    qkv_half, proj_half, tail = kernel_call(
+        finish_mine_kernel, sums + [shape((64, 256))], [spots, *mine], "finish_mine", 10**6,
+        in_specs=[SM] + [HB] * 4, out_specs=[HB, HB, VM], scratch=landing,
     )
     line = shape((768,), F32)
     qkv_sum, proj_sum, *rest = kernel_call(
         finish_other_kernel,
         sums + [line] * 4 + [shape((16,), I32), shape((1, 1, 16), I32)],
-        [place, other, mine[GEMM_ROWS:], qkv_half, proj_half],
+        [spots, tail, *swapped, qkv_half, proj_half],
         "finish_other", 10**6,
-        in_specs=[SM, VM, VM] + away_spec, out_specs=away_spec + [VM] * 6, scratch=landing,
-        aliases={3: 0, 4: 1},
+        in_specs=[SM, VM] + [HB] * 6, out_specs=[HB] * 2 + [VM] * 6, scratch=landing,
+        aliases={6: 0, 7: 1},
     )
     return (
         block_output.reshape(rows3),

time: 302 us -> 304 us (level)
    ppermute x1 -> x6, starting transfers between devices: 6.07 us -> 13 us  [the longest x4 9.72 us: sum_finish(): lax.ppermute(a, 'seq', SWAP)]
    ppermute x2, waiting for transfers between devices: 15.3 us -> 8.78 us  [sum_start(): lax.ppermute(part(i, 1 - bits[i]).astype(BF), BOTH, first_pairs(PAIRS_OF[...]
    ppermute x3, starting transfers between devices: 8.1 us -> 1.75 us  [sum_finish(): lax.ppermute(piece, BOTH, second_step(d))]
    ppermute x1, waiting for transfers between devices: 0.01 us -> 6.22 us  [local(): from_one = lax.ppermute(input_one, 'seq', SWAP)]
    ppermute x4 -> x2, waiting for transfers between devices: 8.16 us -> 3.2 us  [pair_gather(): lax.ppermute(data, BOTH, first_pairs(pair))]
    ppermute x1, waiting for transfers between devices: 4.96 us -> 0.01 us  [local(): got = lax.ppermute(after_all(away, returned), 'seq', SWAP)]
    ppermute x3, waiting for transfers between devices: 0.01 us -> 4.28 us  [sum_finish(): total = total + lax.ppermute(whole, 'seq', along_z(d)).astype(F32)]
  transfers between devices with their start and end apart: 29 -> 32, of which waited for: 14 -> 16; matrix products, arithmetic and copies ran while one was open for 3% -> 5% of each run, Pallas kernels for 38% -> 39%
where the time goes in v1:
time: 304 us; the launch traced here: 300 us
  Pallas kernels  139 us (46%)
  starting transfers between devices  76.3 us (25%)
  waiting for transfers between devices  55.7 us (18%)
  between operations  14.6 us (5%)
  other arithmetic  11.5 us (4%)
    pallas_call x13, Pallas kernels, kernel_call(): pl.pallas_call(body, out_shape=outs, in_specs=in_specs or [VM] * len(args...  139 us
    all_to_all x4, starting transfers between devices, exchange(): lax.all_to_all(array.reshape(16, CAP, 768), 'batch', split_axis=0, concat...  25.2 us
    all_to_all x4, waiting for transfers between devices, exchange(): lax.all_to_all(array.reshape(16, CAP, 768), 'batch', split_axis=0, concat...  11.1 us
    ppermute x4, starting transfers between devices, sum_finish(): lax.ppermute(a, 'seq', SWAP)  9.72 us
    ppermute x2, waiting for transfers between devices, sum_start(): lax.ppermute(part(i, 1 - bits[i]).astype(BF), BOTH, first_pairs(PAIRS_OF[...  8.78 us
    ppermute x3, waiting for transfers between devices, sum_finish(): lax.ppermute(piece, BOTH, second_step(d))  6.46 us
    ppermute x1, waiting for transfers between devices, local(): from_one = lax.ppermute(input_one, 'seq', SWAP)  6.22 us
  transfers between devices with their start and end apart: 32, of which 16 were waited for; matrix products, arithmetic and copies ran while one was open for 5% of the time, Pallas kernels for 39%

profile of v1, /device:TPU:1, one launch (start us, length us, event | category | flops | bytes accessed | tf_op | source)
XLA Modules:
  0.0 300.3 jit_solution(12021955625744886287)
XLA Ops:
  7.2 5.3 %collective-permute-start = (bf16[4,128,768]{2,1,0:T(8,128)(2,1)}, bf16[4,128,768]{2,1,0:T(8,128)(2,1)}, u32[]{:S(2)}, u32[]{:S(2)}) collective-permute-start(bf16[4,128,768]{2,1,0:T(8,128)(2,1)} %x.3), channel_id=1, source_target_pairs={{0,2},{1,3},{2,4},{3,5},{4,6},{5,7},{8,10},{9,11},{10,12},{11,13},... | collective-permute-start | bytes 2359304 | tf_op jit(solution)/shard_map/ppermute | solution.py:637
  12.4 1.4 pad_bitcast_fusion.table
  13.8 0.6 pad_add_fusion.place
  14.4 3.7 %route.1 = (s32[8,512]{1,0:T(8,128)}, f32[16,128]{1,0:T(8,128)}, bf16[1024,768]{1,0:T(8,128)(2,1)}) custom-call(s32[2]{0:T(128)} %pad_add_fusion.place, s32[4,128]{1,0:T(4,128)} %tok.1, s32[64,128]{1,0:T(8,128)} %pad_bitcast_fusion.table, s32[4,128]{1,0:T(4,128)} %turn.5, bf16[512,768]{1,0:T(8,128)(2,1)} %bitcast.87), custom_call_target="tpu_custom_call" | custom-call | flops 1000000000 | bytes 2420744 | tf_op jit(solution)/shard_map/route/pallas_call | solution.py:40
  18.1 6.9 %all-to-all-start.1 = ((bf16[16,64,768]{2,1,0:T(8,128)(2,1)}), bf16[16,64,768]{2,1,0:T(8,128)(2,1)}, u32[]{:S(2)}, u32[]{:S(2)}) async-start(bf16[16,64,768]{2,1,0:T(8,128)(2,1)} %bitcast.65), calls=%async_computation.1 | async-start | bytes 3145728 | tf_op jit(solution)/shard_map/all_to_all | solution.py:620
  25.0 1.3 collective-permute-start.1
  26.3 5.8 %own.1 = (bf16[512,768]{1,0:T(8,128)(2,1)}, bf16[512,768]{1,0:T(8,128)(2,1)}, bf16[512,1536]{1,0:T(8,128)(2,1)}) custom-call(bf16[512,768]{1,0:T(8,128)(2,1)} %bitcast.55, f32[768]{0:T(1024)} %gain.7, f32[768]{0:T(1024)} %bias.5, bf16[768,2304]{1,0:T(8,128)(2,1)} %weight.7), custom_call_target="tpu_custom_call" | custom-call | flops 1800000000 | bytes 7477248 | tf_op jit(solution)/shard_map/own/pallas_call | solution.py:40
  32.1 4.9 %collective-permute-start.2 = (bf16[4,128,768]{2,1,0:T(8,128)(2,1)}, bf16[4,128,768]{2,1,0:T(8,128)(2,1)}, u32[]{:S(2)}, u32[]{:S(2)}) collective-permute-start(bf16[4,128,768]{2,1,0:T(8,128)(2,1)} %collective-permute-done.behind_two), channel_id=1, source_target_pairs={{1,0},{3,2},{5,4},{7,6},{9,8},{11,10},{13,12},{15,14},{17,16},{19,... | collective-permute-start | bytes 2359304 | tf_op jit(solution)/shard_map/ppermute | solution.py:656
  37.1 1.3 collective-permute-done.2.late
  38.4 15.7 %forward.1 = (bf16[4,256,768]{2,1,0:T(8,128)(2,1)}, bf16[4,384,1536]{2,1,0:T(8,128)(2,1)}, bf16[4,128,768]{2,1,0:T(8,128)(2,1)}, f32[4,8,256]{2,1,0:T(8,128)}, f...) custom-call(s32[2]{0:T(128)} %pad_add_fusion.place, s32[4,8]{1,0:T(4,128)} %lengths.3, f32[768]{0:T(1024)} %gain.7, ...), custom_call_target="tpu_custom_call" | custom-call | flops 1000000000 | bytes 20508808 | tf_op jit(solution)/shard_map/forward/pallas_call | solution.py:40
  54.1 7.2 %all-to-all-start = ((bf16[16,64,768]{2,1,0:T(8,128)(2,1)}), bf16[16,64,768]{2,1,0:T(8,128)(2,1)}, u32[]{:S(2)}, u32[]{:S(2)}) async-start(bf16[16,64,768]{2,1,0:T(8,128)(2,1)} %bitcast.66), calls=%async_computation | async-start | bytes 3145728 | tf_op jit(solution)/shard_map/all_to_all | solution.py:620
  61.3 3.8 %turn.4.turned = bf16[784,1536]{1,0:T(8,128)(2,1)} custom-call(bf16[512,768]{1,0:T(8,128)(2,1)} %get-tuple-element.65.unit, bf16[1024,768]{1,0:T(8,128)(2,1)} %bitcast.68), custom_call_target="tpu_custom_call" | custom-call | flops 1000000 | bytes 4767744 | tf_op jit(solution)/shard_map/turn/pallas_call | solution.py:40
  65.1 9.1 %active_grad.1.raw = bf16[4,1024,768]{2,1,0:T(8,128)(2,1)} custom-call(bf16[1024,768]{1,0:T(8,128)(2,1)} %bitcast.10.grad, bf16[3072,768]{1,0:T(8,128)(2,1)} %bitcast.85), custom_call_target="tpu_custom_call" | custom-call | flops 4800000000 | bytes 12582912 | tf_op jit(solution)/shard_map/active_grad/pallas_call | solution.py:40
  74.3 11.1 %all-to-all-done = bf16[16,64,768]{2,1,0:T(8,128)(2,1)} async-done(((bf16[16,64,768]{2,1,0:T(8,128)(2,1)}), bf16[16,64,768]{2,1,0:T(8,128)(2,1)}, u32[]{:S(2)}, u32[]{:S(2)}) %all-to-all-start) | async-done | bytes 1572896 | tf_op jit(solution)/shard_map/all_to_all | solution.py:620
  85.4 16.3 %expert.1 = (bf16[4,1024,768]{2,1,0:T(8,128)(2,1)}, bf16[4,1024,768]{2,1,0:T(8,128)(2,1)}, bf16[1024,768]{1,0:T(8,128)(2,1)}) custom-call(bf16[1024,768]{1,0:T(8,128)(2,1)} %bitcast.8.x, bf16[768,3072]{1,0:T(8,128)(2,1)} %bitcast.84, bf16[4,1024,768]{2,1,0:T(8,128)(2,1)} %active_grad.1.raw), custom_call_target="tpu_custom_call" | custom-call | flops 9699999744 | bytes 26738688 | tf_op jit(solution)/shard_map/expert/pallas_call | solution.py:40
  101.7 4.4 %all-to-all-start.3 = ((bf16[16,64,768]{2,1,0:T(8,128)(2,1)}), bf16[16,64,768]{2,1,0:T(8,128)(2,1)}, u32[]{:S(2)}, u32[]{:S(2)}) async-start(bf16[16,64,768]{2,1,0:T(8,128)(2,1)} %bitcast.67), calls=%async_computation.3 | async-start | bytes 3145728 | tf_op jit(solution)/shard_map/all_to_all | solution.py:620
  106.2 22.3 %weights.1 = (bf16[1024,768]{1,0:T(8,128)(2,1)}, bf16[8,1536,384]{2,1,0:T(8,128)(2,1)}) custom-call(bf16[1024,768]{1,0:T(8,128)(2,1)} %bitcast.8.x, bf16[1024,768]{1,0:T(8,128)(2,1)} %bitcast.10.grad, bf16[4,1024,768]{2,1,0:T(8,128)(2,1)} %get-tuple-element.68.active, bf16[4,1024,768]{2,1,0:T(8,128)(2,1)} %get-tuple-element.69.hidden_grad, ...), custom_call_target="tpu_custom_call" | custom-call | flops 14499999744 | bytes 31457280 | tf_op jit(solution)/shard_map/weights/pallas_call | solution.py:40
  128.5 6.6 %all-to-all-start.2 = ((bf16[16,64,768]{2,1,0:T(8,128)(2,1)}), bf16[16,64,768]{2,1,0:T(8,128)(2,1)}, u32[]{:S(2)}, u32[]{:S(2)}) async-start(bf16[16,64,768]{2,1,0:T(8,128)(2,1)} %bitcast.14), calls=%async_computation.2 | async-start | bytes 3145728 | tf_op jit(solution)/shard_map/all_to_all | solution.py:620
  135.1 36.5 %backward.1 = (f32[512,768]{1,0:T(8,128)}, bf16[512,768]{1,0:T(8,128)(2,1)}, bf16[512,1536]{1,0:T(8,128)(2,1)}, bf16[4,128,768]{2,1,0:T(8,128)(2,1)}, bf16[4,128...) custom-call(s32[2]{0:T(128)} %pad_add_fusion.place, s32[4,8]{1,0:T(4,128)} %lengths.3, ...), custom_call_target="tpu_custom_call" | custom-call | flops 16000000000 | bytes 27905160 | tf_op jit(solution)/shard_map/backward/pallas_call | solution.py:40
  171.7 2.4 collective-permute-start.5
  174.2 6.2 %collective-permute-done.3 = bf16[4,128,768]{2,1,0:T(8,128)(2,1)S(1)} collective-permute-done((bf16[4,128,768]{2,1,0:T(8,128)(2,1)}, bf16[4,128,768]{2,1,0:T(8,128)(2,1)S(1)}, u32[]{:S(2)}, u32[]{:S(2)}) %collective-permute-start.3) | collective-permute-done | bytes 786464 | tf_op jit(solution)/shard_map/ppermute | solution.py:758
  180.4 2.5 add_convert_fusion
  182.9 2.7 collective-permute-start.8
  185.6 8.2 %collective-permute-done.8 = bf16[1216,256]{1,0:T(8,128)(2,1)} collective-permute-done((bf16[1216,256]{1,0:T(8,128)(2,1)}, bf16[1216,256]{1,0:T(8,128)(2,1)}, u32[]{:S(2)}, u32[]{:S(2)}) %collective-permute-start.8) | collective-permute-done | bytes 622624 | tf_op jit(solution)/shard_map/ppermute | solution.py:568
  193.8 3.0 %convert_add_fusion = (f32[1216,256]{1,0:T(8,128)}, bf16[1216,256]{1,0:T(8,128)(2,1)}) fusion(bf16[1216,256]{1,0:T(8,128)(2,1)} %collective-permute-done.8, bf16[4864,256]{1,0:T(8,128)(2,1)S(1)} %collective-permute-done.5, s32[]{:T(128)S(6)} %select_n.138, bf16[4864,256]{1,0:T(8,128)(2,1)} %get-tuple-element.81, s32[]{:T(128)S(6)} %select_n.135), kind=kLoop, calls=%fused_computation | loop fusion | flops 2801664 | bytes 4980744 | tf_op jit(solution)/shard_map/add | solution.py:588
  196.9 0.2 collective-permute-start.6
  197.1 4.0 %output.1 = bf16[512,768]{1,0:T(8,128)(2,1)} custom-call(f32[512,768]{1,0:T(8,128)} %get-tuple-element.63.after, s32[8,512]{1,0:T(8,128)} %get-tuple-element.58.target, bf16[1024,768]{1,0:T(8,128)(2,1)} %bitcast.15.returned), custom_call_target="tpu_custom_call" | custom-call | flops 800000000 | bytes 3948544 | tf_op jit(solution)/shard_map/output/pallas_call | solution.py:40
  201.1 2.2 add_select_fusion
  203.3 1.3 collective-permute-start.4
  204.7 1.3 collective-permute-start.9
  206.0 0.5 collective-permute-done.6
  206.6 1.7 convert_add_fusion.1
  208.2 0.8 dynamic-slice_convert_fusion.1
  209.0 2.7 collective-permute-start.7
  211.7 4.7 %collective-permute-done.7 = bf16[608,256]{1,0:T(8,128)(2,1)S(1)} collective-permute-done((bf16[608,256]{1,0:T(8,128)(2,1)}, bf16[608,256]{1,0:T(8,128)(2,1)S(1)}, u32[]{:S(2)}, u32[]{:S(2)}) %collective-permute-start.7) | collective-permute-done | bytes 311328 | tf_op jit(solution)/shard_map/ppermute | solution.py:591
  216.5 2.9 expert_sum.1
  219.5 3.6 %collective-permute-done.4 = bf16[4,128,768]{2,1,0:T(8,128)(2,1)} collective-permute-done((bf16[4,128,768]{2,1,0:T(8,128)(2,1)}, bf16[4,128,768]{2,1,0:T(8,128)(2,1)}, u32[]{:S(2)}, u32[]{:S(2)}) %collective-permute-start.4) | collective-permute-done | bytes 786464 | tf_op jit(solution)/shard_map/ppermute | solution.py:762
  223.1 2.8 collective-permute-start.12
  226.1 1.3 collective-permute-start.10
  227.4 0.7 collective-permute-done.12
  228.1 5.3 %collective-permute-done.11 = bf16[2,152,256]{2,1,0:T(8,128)(2,1)S(1)} collective-permute-done((bf16[2,152,256]{2,1,0:T(8,128)(2,1)S(1)}, bf16[2,152,256]{2,1,0:T(8,128)(2,1)S(1)}, u32[]{:S(2)}, u32[]{:S(2)}) %collective-permute-start.11) | collective-permute-done | bytes 155680 | tf_op jit(solution)/shard_map/ppermute | solution.py:598
  233.5 0.5 collective-permute-start.15
  234.0 1.0 collective-permute-start.14
  235.0 2.4 collective-permute-start.13
  237.6 1.7 collective-permute-done.14
  239.3 2.4 collective-permute-done.13
  241.8 1.1 collective-permute-start.18
  242.9 0.7 collective-permute-start.16
  243.5 2.5 collective-permute-done.18
  246.1 2.5 collective-permute-done.17
  248.6 1.4 collective-permute-done.16
  250.3 2.4 collective-permute-start.19
  252.7 3.7 %collective-permute-start.21 = (bf16[608,256]{1,0:T(8,128)(2,1)S(1)}, bf16[608,256]{1,0:T(8,128)(2,1)S(1)}, u32[]{:S(2)}, u32[]{:S(2)}) collective-permute-start(bf16[608,256]{1,0:T(8,128)(2,1)S(1)} %bitcast.71), channel_id=1, source_target_pairs={{0,8},{1,33},{2,10},{3,35},{4,12},{5,37},{6,14},{7,39},{8,0},{9,41... | collective-permute-start | bytes 933896 | tf_op jit(solution)/shard_map/ppermute | solution.py:578
  256.3 3.2 %collective-permute-done.19 = bf16[608,256]{1,0:T(8,128)(2,1)S(1)} collective-permute-done((bf16[608,256]{1,0:T(8,128)(2,1)S(1)}, bf16[608,256]{1,0:T(8,128)(2,1)S(1)}, u32[]{:S(2)}, u32[]{:S(2)}) %collective-permute-start.19) | collective-permute-done | bytes 311328 | tf_op jit(solution)/shard_map/ppermute | solution.py:578
  259.7 1.2 collective-permute-start.20
  260.8 0.9 maximum_select_fusion.1
  261.8 2.1 collective-permute-start.22
  263.8 7.8 %input_grad.1 = f32[512,768]{1,0:T(8,128)} custom-call(f32[1]{0:T(128)} %bitcast.17.even, f32[768]{0:T(1024)} %gain.7, bf16[512,768]{1,0:T(8,128)(2,1)} %get-tuple-element.76.query_grad, bf16[512,1536]{1,0:T(8,128)(2,1)} %get-tuple-element.77.own_grad, bf16[768,2304]{1,0:T(8,128)(2,1)} %weight.7, bf16[512,768]{1,0:T(8,128)(2,1)} %bitcast.56, ...), custom_call_target="tpu_custom_call" | custom-call | flops 3000000000 | bytes 11406340 | tf_op jit(solution)/shard_map/input_grad/pallas_call | solution.py:40
  271.6 7.3 %collective-permute-start.23 = (bf16[1216,256]{1,0:T(8,128)(2,1)S(1)}, bf16[1216,256]{1,0:T(8,128)(2,1)}, u32[]{:S(2)}, u32[]{:S(2)}) collective-permute-start(bf16[1216,256]{1,0:T(8,128)(2,1)S(1)} %bitcast.63), channel_id=1, source_target_pairs={{0,1},{1,0},{2,3},{3,2},{4,5},{5,4},{6,7},{7,6},{8,9},{9,8},{10,11... | collective-permute-start | bytes 1867784 | tf_op jit(solution)/shard_map/ppermute | solution.py:611
  279.1 0.4 collective-permute-start.24
  279.5 1.9 collective-permute-start.26
  281.4 0.7 stack.88.place
  282.0 5.4 %finish_mine.1 = (f32[768,2304]{1,0:T(8,128)}, f32[768,768]{1,0:T(8,128)}, bf16[64,256]{1,0:T(8,128)(2,1)}) custom-call(s32[7]{0:T(128)} %stack.88.place, bf16[1216,256]{1,0:T(8,128)(2,1)} %bitcast.64, bf16[1216,256]{1,0:T(8,128)(2,1)} %collective-permute-done.20.b, bf16[1216,256]{1,0:T(8,128)(2,1)} %bitcast.46.c, bf16[1216,256]{1,0:T(8,128)(2,1)} %collective-permute-done.22.d), custom_call_target="tpu_custom_call" | custom-call | flops 1000000 | bytes 11960348 | tf_op jit(solution)/shard_map/finish_mine/pallas_call | solution.py:40
  287.5 5.6 %finish_other.1 = (f32[768,2304]{1,0:T(8,128)}, f32[768,768]{1,0:T(8,128)}, f32[768]{0:T(1024)}, f32[768]{0:T(1024)}, f32[768]{0:T(1024)}, /*index=5*/f32[768]{0:T(1024)}, s32[16]{0:T(128)}, s32[1,1,16]{2,1,0:T(1,128)}) custom-call(s32[7]{0:T(128)} %stack.88.place, ...), custom_call_target="tpu_custom_call", output_to_operand_aliasing={{0}: (6, {}), {1}: (7, {})} | custom-call | flops 1000000 | bytes 21409948 | tf_op jit(solution)/shard_map/finish_other/pallas_call | solution.py:40
  (44 shorter events, 1.5 us)
Async XLA Ops:
  7.2 25.0 %collective-permute-start = (bf16[4,128,768]{2,1,0:T(8,128)(2,1)}, bf16[4,128,768]{2,1,0:T(8,128)(2,1)}, u32[]{:S(2)}, u32[]{:S(2)}) collective-permute-start(bf16[4,128,768]{2,1,0:T(8,128)(2,1)} %x.3), channel_id=1, source_target_pairs={{0,2},{1,3},{2,4},{3,5},{4,6},{5,7},{8,10},{9,11},{10,12},{11,13},... | collective-permute-start | bytes 2359304 | tf_op jit(solution)/shard_map/ppermute | solution.py:637
  18.1 6.9 %copy-start.1 = (bf16[4,128,768]{2,1,0:T(8,128)(2,1)S(1)}, bf16[4,128,768]{2,1,0:T(8,128)(2,1)}, u32[]{:S(2)}) copy-start(bf16[4,128,768]{2,1,0:T(8,128)(2,1)} %x.3) | copy-start | bytes 2359300
  18.1 36.0 %all-to-all-start.1 = ((bf16[16,64,768]{2,1,0:T(8,128)(2,1)}), bf16[16,64,768]{2,1,0:T(8,128)(2,1)}, u32[]{:S(2)}, u32[]{:S(2)}) async-start(bf16[16,64,768]{2,1,0:T(8,128)(2,1)} %bitcast.65), calls=%async_computation.1 | async-start | bytes 3145728 | tf_op jit(solution)/shard_map/all_to_all | solution.py:620
  25.0 12.0 %collective-permute-start.1 = (bf16[4,128,768]{2,1,0:T(8,128)(2,1)S(1)}, bf16[4,128,768]{2,1,0:T(8,128)(2,1)}, u32[]{:S(2)}, u32[]{:S(2)}) collective-permute-start(bf16[4,128,768]{2,1,0:T(8,128)(2,1)S(1)} %copy-done.1), channel_id=1, source_target_pairs={{0,1},{2,3},{4,5},{6,7},{8,9},{10,11},{12,13},{14,15},{16,17},{18,... | collective-permute-start | bytes 2359304 | tf_op jit(solution)/shard_map/ppermute | solution.py:638
  32.1 6.2 %collective-permute-start.2 = (bf16[4,128,768]{2,1,0:T(8,128)(2,1)}, bf16[4,128,768]{2,1,0:T(8,128)(2,1)}, u32[]{:S(2)}, u32[]{:S(2)}) collective-permute-start(bf16[4,128,768]{2,1,0:T(8,128)(2,1)} %collective-permute-done.behind_two), channel_id=1, source_target_pairs={{1,0},{3,2},{5,4},{7,6},{9,8},{11,10},{13,12},{15,14},{17,16},{19,... | collective-permute-start | bytes 2359304 | tf_op jit(solution)/shard_map/ppermute | solution.py:656
  54.1 31.2 %all-to-all-start = ((bf16[16,64,768]{2,1,0:T(8,128)(2,1)}), bf16[16,64,768]{2,1,0:T(8,128)(2,1)}, u32[]{:S(2)}, u32[]{:S(2)}) async-start(bf16[16,64,768]{2,1,0:T(8,128)(2,1)} %bitcast.66), calls=%async_computation | async-start | bytes 3145728 | tf_op jit(solution)/shard_map/all_to_all | solution.py:620
  101.7 26.8 %all-to-all-start.3 = ((bf16[16,64,768]{2,1,0:T(8,128)(2,1)}), bf16[16,64,768]{2,1,0:T(8,128)(2,1)}, u32[]{:S(2)}, u32[]{:S(2)}) async-start(bf16[16,64,768]{2,1,0:T(8,128)(2,1)} %bitcast.67), calls=%async_computation.3 | async-start | bytes 3145728 | tf_op jit(solution)/shard_map/all_to_all | solution.py:620
  106.2 110.4 %reduce-scatter.2.cloned.1.call-start = ((), (), s32[]{:S(2)}) async-start(), calls=%async_computation.5 | async-start | bytes 10616832 | tf_op jit(solution)/shard_map/reduce_scatter | solution.py:730
  128.5 43.2 %all-to-all-start.2 = ((bf16[16,64,768]{2,1,0:T(8,128)(2,1)}), bf16[16,64,768]{2,1,0:T(8,128)(2,1)}, u32[]{:S(2)}, u32[]{:S(2)}) async-start(bf16[16,64,768]{2,1,0:T(8,128)(2,1)} %bitcast.14), calls=%async_computation.2 | async-start | bytes 3145728 | tf_op jit(solution)/shard_map/all_to_all | solution.py:620
  171.7 8.7 %collective-permute-start.5 = (bf16[4864,256]{1,0:T(8,128)(2,1)}, bf16[4864,256]{1,0:T(8,128)(2,1)S(1)}, u32[]{:S(2)}, u32[]{:S(2)}) collective-permute-start(bf16[4864,256]{1,0:T(8,128)(2,1)} %get-tuple-element.83), channel_id=1, source_target_pairs={{0,1},{1,0},{2,3},{3,2},{4,5},{5,4},{6,7},{7,6},{8,9},{9,8},{10,11... | collective-permute-start | bytes 7471112 | tf_op jit(solution)/shard_map/ppermute | solution.py:757
  174.1 6.3 %collective-permute-start.3 = (bf16[4,128,768]{2,1,0:T(8,128)(2,1)}, bf16[4,128,768]{2,1,0:T(8,128)(2,1)S(1)}, u32[]{:S(2)}, u32[]{:S(2)}) collective-permute-start(bf16[4,128,768]{2,1,0:T(8,128)(2,1)} %get-tuple-element.78), channel_id=1, source_target_pairs={{0,1},{1,0},{2,3},{3,2},{4,5},{5,4},{6,7},{7,6},{8,9},{9,8},{10,11... | collective-permute-start | bytes 2359304 | tf_op jit(solution)/shard_map/ppermute | solution.py:758
  180.4 20.7 %copy-start.2 = (bf16[4,128,768]{2,1,0:T(8,128)(2,1)}, bf16[4,128,768]{2,1,0:T(8,128)(2,1)S(1)}, u32[]{:S(2)}) copy-start(bf16[4,128,768]{2,1,0:T(8,128)(2,1)S(1)} %collective-permute-done.3) | copy-start | bytes 2359300
  180.4 16.4 %copy-start.3 = (bf16[4864,256]{1,0:T(8,128)(2,1)}, bf16[4864,256]{1,0:T(8,128)(2,1)S(1)}, u32[]{:S(2)}) copy-start(bf16[4864,256]{1,0:T(8,128)(2,1)S(1)} %collective-permute-done.5) | copy-start | bytes 7471108
  182.9 10.9 %collective-permute-start.8 = (bf16[1216,256]{1,0:T(8,128)(2,1)}, bf16[1216,256]{1,0:T(8,128)(2,1)}, u32[]{:S(2)}, u32[]{:S(2)}) collective-permute-start(bf16[1216,256]{1,0:T(8,128)(2,1)} %add_convert_fusion), channel_id=1, source_target_pairs={{0,24},{1,97},{2,26},{3,99},{4,28},{5,101},{6,30},{7,103},{8,16},{... | collective-permute-start | bytes 1867784 | tf_op jit(solution)/shard_map/ppermute | solution.py:568
  196.9 9.7 %collective-permute-start.6 = (bf16[1216,256]{1,0:T(8,128)(2,1)}, bf16[1216,256]{1,0:T(8,128)(2,1)}, u32[]{:S(2)}, u32[]{:S(2)}) collective-permute-start(bf16[1216,256]{1,0:T(8,128)(2,1)} %get-tuple-element.105), channel_id=1, source_target_pairs={{0,8},{1,33},{2,10},{3,35},{4,12},{5,37},{6,14},{7,39},{8,0},{9,41... | collective-permute-start | bytes 1867784 | tf_op jit(solution)/shard_map/ppermute | solution.py:568
  201.1 3.5 %copy-start = (f32[1216,256]{1,0:T(8,128)S(1)}, f32[1216,256]{1,0:T(8,128)}, u32[]{:S(2)}) copy-start(f32[1216,256]{1,0:T(8,128)} %get-tuple-element.104) | copy-start | bytes 3735556
  203.3 19.8 %collective-permute-start.4 = (bf16[4,128,768]{2,1,0:T(8,128)(2,1)}, bf16[4,128,768]{2,1,0:T(8,128)(2,1)}, u32[]{:S(2)}, u32[]{:S(2)}) collective-permute-start(bf16[4,128,768]{2,1,0:T(8,128)(2,1)} %add_select_fusion), channel_id=1, source_target_pairs={{2,0},{3,1},{4,2},{5,3},{6,4},{7,5},{10,8},{11,9},{12,10},{13,11},... | collective-permute-start | bytes 2359304 | tf_op jit(solution)/shard_map/ppermute | solution.py:762
  204.7 7.0 %collective-permute-start.9 = (bf16[608,256]{1,0:T(8,128)(2,1)S(1)}, bf16[608,256]{1,0:T(8,128)(2,1)S(1)}, u32[]{:S(2)}, u32[]{:S(2)}) collective-permute-start(bf16[608,256]{1,0:T(8,128)(2,1)S(1)} %dynamic-slice_convert_fusion), channel_id=1, source_target_pairs={{0,8},{1,33},{2,10},{3,35},{4,12},{5,37},{6,14},{7,39},{8,0},{9,41... | collective-permute-start | bytes 933896 | tf_op jit(solution)/shard_map/ppermute | solution.py:591
  209.0 7.5 %collective-permute-start.7 = (bf16[608,256]{1,0:T(8,128)(2,1)}, bf16[608,256]{1,0:T(8,128)(2,1)S(1)}, u32[]{:S(2)}, u32[]{:S(2)}) collective-permute-start(bf16[608,256]{1,0:T(8,128)(2,1)} %dynamic-slice_convert_fusion.1), channel_id=1, source_target_pairs={{0,24},{1,97},{2,26},{3,99},{4,28},{5,101},{6,30},{7,103},{8,16},{... | collective-permute-start | bytes 933896 | tf_op jit(solution)/shard_map/ppermute | solution.py:591
  223.1 5.0 %collective-permute-start.12 = (bf16[2,152,256]{2,1,0:T(8,128)(2,1)S(1)}, bf16[2,152,256]{2,1,0:T(8,128)(2,1)S(1)}, u32[]{:S(2)}, u32[]{:S(2)}) collective-permute-start(bf16[2,152,256]{2,1,0:T(8,128)(2,1)S(1)} %get-tuple-element.114), channel_id=1, source_target_pairs={{0,96},{1,25},{2,98},{3,27},{4,100},{5,29},{6,102},{7,31},{8,104},... | collective-permute-start | bytes 466952 | tf_op jit(solution)/shard_map/ppermute | solution.py:598
  225.9 7.4 %collective-permute-start.11 = (bf16[2,152,256]{2,1,0:T(8,128)(2,1)S(1)}, bf16[2,152,256]{2,1,0:T(8,128)(2,1)S(1)}, u32[]{:S(2)}, u32[]{:S(2)}) collective-permute-start(bf16[2,152,256]{2,1,0:T(8,128)(2,1)S(1)} %get-tuple-element.113), channel_id=1, source_target_pairs={{0,32},{1,9},{2,34},{3,11},{4,36},{5,13},{6,38},{7,15},{8,40},{9,1... | collective-permute-start | bytes 466952 | tf_op jit(solution)/shard_map/ppermute | solution.py:598
  226.1 7.2 %collective-permute-start.10 = (bf16[2,152,256]{2,1,0:T(8,128)(2,1)S(1)}, bf16[2,152,256]{2,1,0:T(8,128)(2,1)S(1)}, u32[]{:S(2)}, u32[]{:S(2)}) collective-permute-start(bf16[2,152,256]{2,1,0:T(8,128)(2,1)S(1)} %get-tuple-element.112), channel_id=1, source_target_pairs={{0,64},{1,17},{2,66},{3,19},{4,68},{5,21},{6,70},{7,23},{8,72},{9,... | collective-permute-start | bytes 466952 | tf_op jit(solution)/shard_map/ppermute | solution.py:598
  233.5 4.2 %collective-permute-start.15 = (bf16[2,152,256]{2,1,0:T(8,128)(2,1)S(1)}, bf16[2,152,256]{2,1,0:T(8,128)(2,1)S(1)}, u32[]{:S(2)}, u32[]{:S(2)}) collective-permute-start(bf16[2,152,256]{2,1,0:T(8,128)(2,1)S(1)} %fusion.2), channel_id=1, source_target_pairs={{0,6},{1,7},{2,0},{3,1},{4,2},{5,3},{6,4},{7,5},{8,14},{9,15},{10,... | collective-permute-start | bytes 466952 | tf_op jit(solution)/shard_map/ppermute | solution.py:602
  234.0 5.3 %collective-permute-start.14 = (bf16[2,152,256]{2,1,0:T(8,128)(2,1)S(1)}, bf16[2,152,256]{2,1,0:T(8,128)(2,1)S(1)}, u32[]{:S(2)}, u32[]{:S(2)}) collective-permute-start(bf16[2,152,256]{2,1,0:T(8,128)(2,1)S(1)} %fusion.2), channel_id=1, source_target_pairs={{0,2},{1,3},{2,4},{3,5},{4,6},{5,7},{6,0},{7,1},{8,10},{9,11},{10,... | collective-permute-start | bytes 466952 | tf_op jit(solution)/shard_map/ppermute | solution.py:602
  235.0 6.7 %collective-permute-start.13 = (bf16[2,152,256]{2,1,0:T(8,128)(2,1)S(1)}, bf16[2,152,256]{2,1,0:T(8,128)(2,1)S(1)}, u32[]{:S(2)}, u32[]{:S(2)}) collective-permute-start(bf16[2,152,256]{2,1,0:T(8,128)(2,1)S(1)} %fusion.2), channel_id=1, source_target_pairs={{0,4},{1,5},{2,6},{3,7},{4,0},{5,1},{6,2},{7,3},{8,12},{9,13},{10,... | collective-permute-start | bytes 466952 | tf_op jit(solution)/shard_map/ppermute | solution.py:602
  241.8 4.3 %collective-permute-start.18 = (bf16[2,152,256]{2,1,0:T(8,128)(2,1)S(1)}, bf16[2,152,256]{2,1,0:T(8,128)(2,1)S(1)}, u32[]{:S(2)}, u32[]{:S(2)}) collective-permute-start(bf16[2,152,256]{2,1,0:T(8,128)(2,1)S(1)} %add_convert_fusion.4), channel_id=1, source_target_pairs={{0,96},{1,25},{2,98},{3,27},{4,100},{5,29},{6,102},{7,31},{8,104},... | collective-permute-start | bytes 466952 | tf_op jit(solution)/shard_map/ppermute | solution.py:604
  242.9 5.7 %collective-permute-start.17 = (bf16[2,152,256]{2,1,0:T(8,128)(2,1)S(1)}, bf16[2,152,256]{2,1,0:T(8,128)(2,1)S(1)}, u32[]{:S(2)}, u32[]{:S(2)}) collective-permute-start(bf16[2,152,256]{2,1,0:T(8,128)(2,1)S(1)} %add_convert_fusion.4), channel_id=1, source_target_pairs={{0,64},{1,17},{2,66},{3,19},{4,68},{5,21},{6,70},{7,23},{8,72},{9,... | collective-permute-start | bytes 466952 | tf_op jit(solution)/shard_map/ppermute | solution.py:604
  242.9 7.1 %collective-permute-start.16 = (bf16[2,152,256]{2,1,0:T(8,128)(2,1)S(1)}, bf16[2,152,256]{2,1,0:T(8,128)(2,1)S(1)}, u32[]{:S(2)}, u32[]{:S(2)}) collective-permute-start(bf16[2,152,256]{2,1,0:T(8,128)(2,1)S(1)} %add_convert_fusion.4), channel_id=1, source_target_pairs={{0,32},{1,9},{2,34},{3,11},{4,36},{5,13},{6,38},{7,15},{8,40},{9,1... | collective-permute-start | bytes 466952 | tf_op jit(solution)/shard_map/ppermute | solution.py:604
  250.3 9.3 %collective-permute-start.19 = (bf16[608,256]{1,0:T(8,128)(2,1)S(1)}, bf16[608,256]{1,0:T(8,128)(2,1)S(1)}, u32[]{:S(2)}, u32[]{:S(2)}) collective-permute-start(bf16[608,256]{1,0:T(8,128)(2,1)S(1)} %bitcast.73), channel_id=1, source_target_pairs={{0,24},{1,97},{2,26},{3,99},{4,28},{5,101},{6,30},{7,103},{8,16},{... | collective-permute-start | bytes 933896 | tf_op jit(solution)/shard_map/ppermute | solution.py:578
  252.7 8.2 %collective-permute-start.21 = (bf16[608,256]{1,0:T(8,128)(2,1)S(1)}, bf16[608,256]{1,0:T(8,128)(2,1)S(1)}, u32[]{:S(2)}, u32[]{:S(2)}) collective-permute-start(bf16[608,256]{1,0:T(8,128)(2,1)S(1)} %bitcast.71), channel_id=1, source_target_pairs={{0,8},{1,33},{2,10},{3,35},{4,12},{5,37},{6,14},{7,39},{8,0},{9,41... | collective-permute-start | bytes 933896 | tf_op jit(solution)/shard_map/ppermute | solution.py:578
  259.6 12.0 %copy-start.4 = (bf16[2,608,256]{2,1,0:T(8,128)(2,1)}, bf16[2,608,256]{2,1,0:T(8,128)(2,1)S(1)}, u32[]{:S(2)}) copy-start(bf16[2,608,256]{2,1,0:T(8,128)(2,1)S(1)} %maximum_select_fusion) | copy-start | bytes 1867780
  259.7 19.4 %collective-permute-start.20 = (bf16[1216,256]{1,0:T(8,128)(2,1)S(1)}, bf16[1216,256]{1,0:T(8,128)(2,1)}, u32[]{:S(2)}, u32[]{:S(2)}) collective-permute-start(bf16[1216,256]{1,0:T(8,128)(2,1)S(1)} %bitcast.62), channel_id=1, source_target_pairs={{0,8},{1,33},{2,10},{3,35},{4,12},{5,37},{6,14},{7,39},{8,0},{9,41... | collective-permute-start | bytes 1867784 | tf_op jit(solution)/shard_map/ppermute | solution.py:608
  261.8 17.7 %collective-permute-start.22 = (bf16[1216,256]{1,0:T(8,128)(2,1)}, bf16[1216,256]{1,0:T(8,128)(2,1)}, u32[]{:S(2)}, u32[]{:S(2)}) collective-permute-start(bf16[1216,256]{1,0:T(8,128)(2,1)} %bitcast.46.c), channel_id=1, source_target_pairs={{0,24},{1,97},{2,26},{3,99},{4,28},{5,101},{6,30},{7,103},{8,16},{... | collective-permute-start | bytes 1867784 | tf_op jit(solution)/shard_map/ppermute | solution.py:608
  271.6 15.9 %collective-permute-start.23 = (bf16[1216,256]{1,0:T(8,128)(2,1)S(1)}, bf16[1216,256]{1,0:T(8,128)(2,1)}, u32[]{:S(2)}, u32[]{:S(2)}) collective-permute-start(bf16[1216,256]{1,0:T(8,128)(2,1)S(1)} %bitcast.63), channel_id=1, source_target_pairs={{0,1},{1,0},{2,3},{3,2},{4,5},{5,4},{6,7},{7,6},{8,9},{9,8},{10,11... | collective-permute-start | bytes 1867784 | tf_op jit(solution)/shard_map/ppermute | solution.py:611
  279.0 8.6 %collective-permute-start.25 = (bf16[1216,256]{1,0:T(8,128)(2,1)}, bf16[1216,256]{1,0:T(8,128)(2,1)}, u32[]{:S(2)}, u32[]{:S(2)}) collective-permute-start(bf16[1216,256]{1,0:T(8,128)(2,1)} %bitcast.46.c), channel_id=1, source_target_pairs={{0,1},{1,0},{2,3},{3,2},{4,5},{5,4},{6,7},{7,6},{8,9},{9,8},{10,11... | collective-permute-start | bytes 1867784 | tf_op jit(solution)/shard_map/ppermute | solution.py:611
  279.1 8.5 %collective-permute-start.24 = (bf16[1216,256]{1,0:T(8,128)(2,1)}, bf16[1216,256]{1,0:T(8,128)(2,1)}, u32[]{:S(2)}, u32[]{:S(2)}) collective-permute-start(bf16[1216,256]{1,0:T(8,128)(2,1)} %collective-permute-done.20.b), channel_id=1, source_target_pairs={{0,1},{1,0},{2,3},{3,2},{4,5},{5,4},{6,7},{7,6},{8,9},{9,8},{10,11... | collective-permute-start | bytes 1867784 | tf_op jit(solution)/shard_map/ppermute | solution.py:611
  279.5 8.1 %collective-permute-start.26 = (bf16[1216,256]{1,0:T(8,128)(2,1)}, bf16[1216,256]{1,0:T(8,128)(2,1)}, u32[]{:S(2)}, u32[]{:S(2)}) collective-permute-start(bf16[1216,256]{1,0:T(8,128)(2,1)} %collective-permute-done.22.d), channel_id=1, source_target_pairs={{0,1},{1,0},{2,3},{3,2},{4,5},{5,4},{6,7},{7,6},{8,9},{9,8},{10,11... | collective-permute-start | bytes 1867784 | tf_op jit(solution)/shard_map/ppermute | solution.py:611
Sparse Core Ops, SparseCore 0:
  128.7 59.1 reduce-scatter.1
